TPU v7x, 32 devices: a whole 2x2x4 slice. The times are simulated.
32 devices in a mesh: ctx: 8 (over z, core), wa: 4 (over y, x).
Axes of the slice: x: 2, y: 2, z: 4, core: 2. Of those that a mesh axis runs over, the one named last changes fastest.
Arguments:
- hidden_in: bfloat16 [4096, 576], P('ctx'), may hold values from -6 to 6
- pair_table: int32 [16], replicated, may hold values from 0 to 15, each once
- norm1_gain: bfloat16 [2, 576], replicated, may hold values from 0.099609375 to 1.8984375
- qkv_weight: bfloat16 [2, 576, 960], P(None, 'wa'), may hold values from -0.25 to 0.25
- out_weight: bfloat16 [2, 576, 576], P(None, 'wa'), may hold values from -4 to 4
- norm2_gain: bfloat16 [2, 576], replicated, may hold values from 0.099609375 to 1.8984375
- gate_up_weight: bfloat16 [2, 2, 576, 1536], P(None, None, None, 'wa'), may hold values from -0.25 to 0.25
- down_weight: bfloat16 [2, 1536, 576], P(None, 'wa'), may hold values from -0.15625 to 0.15625
- out_grad: bfloat16 [4096, 576], P('ctx'), may hold values from -6 to 6
Outputs:
- hidden_out: float32 [4096, 576], P('ctx')
- input_grad: float32 [4096, 576], P('ctx')
- norm1_gain_grad: float32 [2, 576], replicated
- qkv_weight_grad: float32 [2, 576, 960], P(None, 'wa')
- out_weight_grad: float32 [2, 576, 576], P(None, 'wa')
- norm2_gain_grad: float32 [2, 576], replicated
- gate_up_weight_grad: float32 [2, 2, 576, 1536], P(None, None, None, 'wa')
- down_weight_grad: float32 [2, 1536, 576], P(None, 'wa')
Inputs may be any that keep to these rules, and one draw needn't show every extreme that they name: `pair_table`: each pair number stands once; slot s lies on index s // 2 of ctx.
All inputs are finite; a program needn't handle non-finite values.
Results may differ from a plain program's by a relative error of at most 0.04.
Values may be sent and summed in bfloat16 or wider, within the bound.
A program may use at most 128 MiB of HBM per device.

v0:
```python
import jax
import jax.numpy as jnp
from jax import lax
from jax.sharding import PartitionSpec as P

QUERY_HEADS = 9
KEY_VALUE_HEADS = 3
HEAD_SIZE = 64
BLK = 128
LAYERS = 2


EPSILON = 1e-05
shards_per_step = 8


def rotation(token_pos, head_width):
    half_width = head_width // 2
    inv_freq = jnp.power(
        jnp.float32(100000.0), -2.0 * jnp.arange(half_width, dtype=jnp.float32) / head_width
    )
    angles = token_pos.astype(jnp.float32)[..., None] * inv_freq
    return (jnp.cos(angles), jnp.sin(angles))


def apply_rotary(vectors, cosine, sine):
    half_width = vectors.shape[-1] // 2
    first_half = vectors[..., :half_width]
    second_half = vectors[..., half_width:]
    cosine = cosine[..., None, :]
    sine = sine[..., None, :]
    return jnp.concatenate(
        [first_half * cosine - second_half * sine, second_half * cosine + first_half * sine],
        axis=-1,
    )


def contract_rows(left, right):
    return lax.dot_general(
        left, right, (((0,), (0,)), ((), ())), preferred_element_type=jnp.float32
    )


def contract_cols(left, right):
    return lax.dot_general(
        left, right, (((1,), (1,)), ((), ())), preferred_element_type=jnp.float32
    )


def width_sum(partial_value):
    return lax.psum(partial_value.astype(jnp.bfloat16), "wa").astype(jnp.float32)


def norm_backward(grad_normed, source, inv_root, gain_row):
    gain_grad = jnp.sum(grad_normed * source * inv_root, axis=0)
    weighted = grad_normed * gain_row
    back = inv_root * (
        weighted
        - source * inv_root * inv_root * jnp.mean(weighted * source, axis=-1, keepdims=True)
    )
    return (gain_grad, back)


def score_block(query_quad, key_blk, key_at, query_pos, score_scale):
    raw = jnp.einsum("qgrd,kgd->grqk", query_quad, key_blk, preferred_element_type=jnp.float32)
    live = key_at[None, None, None, :] <= query_pos[None, None, :, None]
    return (raw * score_scale, live)


def attend_forward(query_quad, key_per_step, value_per_step, key_pos, query_pos, score_scale):
    stat_shape = (query_quad.shape[1], query_quad.shape[2], query_quad.shape[0])

    def first_pass(carry, slice_in):
        running_max, running_sum = carry
        key_blk, key_at = slice_in
        scaled, live = score_block(query_quad, key_blk, key_at, query_pos, score_scale)
        masked = jnp.where(live, scaled, -1e30)
        new_max = jnp.maximum(running_max, jnp.max(masked, axis=-1))
        running_sum = running_sum * jnp.exp(running_max - new_max) + jnp.sum(
            jnp.exp(masked - new_max[..., None]), axis=-1
        )
        return ((new_max, running_sum), None)

    initial = (jnp.full(stat_shape, -1e30, jnp.float32), jnp.zeros(stat_shape, jnp.float32))
    (running_max, running_sum), unused = lax.scan(first_pass, initial, (key_per_step, key_pos))
    log_total = running_max + jnp.log(running_sum)

    def second_pass(weighted, slice_in):
        key_blk, value_blk, key_at = slice_in
        scaled, live = score_block(query_quad, key_blk, key_at, query_pos, score_scale)
        probability = jnp.where(live, jnp.exp(scaled - log_total[..., None]), 0.0).astype(
            jnp.bfloat16
        )
        return (
            weighted
            + jnp.einsum(
                "grqk,kgd->qgrd", probability, value_blk, preferred_element_type=jnp.float32
            ),
            None,
        )

    weighted, unused = lax.scan(
        second_pass,
        jnp.zeros(query_quad.shape, jnp.float32),
        (key_per_step, value_per_step, key_pos),
    )
    return (weighted, log_total)


def attend_backward(
    query_quad,
    gradient_quad,
    weighted,
    key_per_step,
    value_per_step,
    key_pos,
    query_pos,
    log_total,
    score_scale,
):
    delta = jnp.einsum("qgrd,qgrd->grq", gradient_quad.astype(jnp.float32), weighted)

    def second_pass(dquery, slice_in):
        key_blk, value_blk, key_at = slice_in
        scaled, live = score_block(query_quad, key_blk, key_at, query_pos, score_scale)
        probability = jnp.where(live, jnp.exp(scaled - log_total[..., None]), 0.0)
        dprob = jnp.einsum(
            "qgrd,kgd->grqk", gradient_quad, value_blk, preferred_element_type=jnp.float32
        )
        dscore = (probability * (dprob - delta[..., None]) * score_scale).astype(jnp.bfloat16)
        dquery = dquery + jnp.einsum(
            "grqk,kgd->qgrd", dscore, key_blk, preferred_element_type=jnp.float32
        )
        dkey = jnp.einsum("grqk,qgrd->kgd", dscore, query_quad, preferred_element_type=jnp.float32)
        dvalue = jnp.einsum(
            "grqk,qgrd->kgd",
            probability.astype(jnp.bfloat16),
            gradient_quad,
            preferred_element_type=jnp.float32,
        )
        return (dquery, (dkey, dvalue))

    dquery, (key_gradients, dvalues) = lax.scan(
        second_pass,
        jnp.zeros(query_quad.shape, jnp.float32),
        (key_per_step, value_per_step, key_pos),
    )
    return (dquery, key_gradients, dvalues)


def per_device(
    hidden_in,
    pair_table,
    norm1_gain,
    qkv_weight,
    out_weight,
    norm2_gain,
    gate_up_weight,
    down_weight,
    out_grad,
):
    ctx_count = lax.axis_size("ctx")
    wa_count = lax.axis_size("wa")
    ctx_at = lax.axis_index("ctx")
    wa_at = lax.axis_index("wa")
    row_count, hidden_width = hidden_in.shape
    pairs_total = pair_table.shape[0]
    blocks_dev = row_count // BLK
    sub_rows = BLK // wa_count
    local_rows = blocks_dev * sub_rows
    col_width = hidden_width // wa_count
    head_cluster = QUERY_HEADS // KEY_VALUE_HEADS
    key_value_width = KEY_VALUE_HEADS * HEAD_SIZE
    score_scale = HEAD_SIZE ** (-0.5)
    total_step_count = ctx_count * wa_count // shards_per_step
    seq_blocks = jnp.stack([pair_table, 2 * pairs_total - 1 - pair_table], axis=1).reshape(
        ctx_count, blocks_dev
    )
    local_blocks = lax.dynamic_index_in_dim(seq_blocks, ctx_at, 0, keepdims=False)
    sub_iota = jnp.arange(sub_rows, dtype=jnp.int32)
    wa_iota = jnp.arange(wa_count, dtype=jnp.int32)
    own_pos = (local_blocks[:, None] * BLK + wa_at * sub_rows + sub_iota[None, :]).reshape(
        local_rows
    )
    key_pos = (
        seq_blocks[:, None, :, None] * BLK
        + wa_iota[None, :, None, None] * sub_rows
        + sub_iota[None, None, None, :]
    ).reshape(total_step_count, -1)
    local_cosine, local_sine = rotation(own_pos, HEAD_SIZE)
    residual = hidden_in.astype(jnp.float32)
    stored = []
    for layer_at in range(LAYERS):
        gain_one = norm1_gain[layer_at].astype(jnp.float32)
        inv_one = lax.rsqrt(jnp.mean(residual * residual, axis=-1, keepdims=True) + EPSILON)
        normed = (residual * inv_one * gain_one).astype(jnp.bfloat16)
        normed_cols = lax.dynamic_slice_in_dim(normed, wa_at * col_width, col_width, 1)
        partial_value = jnp.dot(
            normed_cols, qkv_weight[layer_at], preferred_element_type=jnp.float32
        )
        local_query_key_value = lax.psum_scatter(
            partial_value.reshape(blocks_dev, wa_count, sub_rows, -1).astype(jnp.bfloat16),
            "wa",
            scatter_dimension=1,
            tiled=True,
        ).astype(jnp.float32)
        local_query_key_value = local_query_key_value.reshape(local_rows, -1)
        query_rows = apply_rotary(
            local_query_key_value[:, :hidden_width].reshape(local_rows, QUERY_HEADS, HEAD_SIZE),
            local_cosine,
            local_sine,
        ).astype(jnp.bfloat16)
        key_matrix_rows = (
            apply_rotary(
                local_query_key_value[:, hidden_width : hidden_width + key_value_width].reshape(
                    local_rows, KEY_VALUE_HEADS, HEAD_SIZE
                ),
                local_cosine,
                local_sine,
            )
            .astype(jnp.bfloat16)
            .reshape(1, local_rows, key_value_width)
        )
        value_matrix_rows = (
            local_query_key_value[:, hidden_width + key_value_width :]
            .astype(jnp.bfloat16)
            .reshape(1, local_rows, key_value_width)
        )
        key_matrix_rows, value_matrix_rows = (
            lax.all_gather(key_matrix_rows, ("ctx", "wa"), axis=0, tiled=True),
            lax.all_gather(value_matrix_rows, ("ctx", "wa"), axis=0, tiled=True),
        )
        key_per_step = key_matrix_rows.reshape(total_step_count, -1, KEY_VALUE_HEADS, HEAD_SIZE)
        value_per_step = value_matrix_rows.reshape(total_step_count, -1, KEY_VALUE_HEADS, HEAD_SIZE)
        query_quad = query_rows.reshape(local_rows, KEY_VALUE_HEADS, head_cluster, HEAD_SIZE)
        weighted, log_total = attend_forward(
            query_quad, key_per_step, value_per_step, key_pos, own_pos, score_scale
        )
        attended = weighted.reshape(local_rows, hidden_width).astype(jnp.bfloat16)
        att_cols = lax.all_to_all(
            attended.reshape(blocks_dev, 1, sub_rows, hidden_width),
            "wa",
            split_axis=3,
            concat_axis=1,
            tiled=True,
        )
        att_cols = att_cols.reshape(row_count, col_width)
        middle = residual + width_sum(
            jnp.dot(att_cols, out_weight[layer_at], preferred_element_type=jnp.float32)
        )
        gain_two = norm2_gain[layer_at].astype(jnp.float32)
        inv_two = lax.rsqrt(jnp.mean(middle * middle, axis=-1, keepdims=True) + EPSILON)
        normed_two = (middle * inv_two * gain_two).astype(jnp.bfloat16)
        gate_pre = jnp.dot(
            normed_two, gate_up_weight[layer_at, 0], preferred_element_type=jnp.float32
        )
        up_proj = jnp.dot(
            normed_two, gate_up_weight[layer_at, 1], preferred_element_type=jnp.float32
        )
        activated = (jax.nn.silu(gate_pre) * up_proj).astype(jnp.bfloat16)
        output_rows = middle + width_sum(
            jnp.dot(activated, down_weight[layer_at], preferred_element_type=jnp.float32)
        )
        stored.append(
            (
                residual,
                inv_one,
                gain_one,
                normed_cols,
                query_quad,
                key_per_step,
                value_per_step,
                log_total,
                weighted,
                att_cols,
                middle,
                inv_two,
                gain_two,
                normed_two,
                gate_pre,
                up_proj,
                activated,
            )
        )
        residual = output_rows
    gradient = out_grad.astype(jnp.float32)
    gain_one_grads = [None] * LAYERS
    qkv_grads = [None] * LAYERS
    out_grads = [None] * LAYERS
    gain_two_grads = [None] * LAYERS
    gate_up_grads = [None] * LAYERS
    down_grads = [None] * LAYERS
    for layer_at in reversed(range(LAYERS)):
        (
            layer_input,
            inv_one,
            gain_one,
            normed_cols,
            query_quad,
            key_per_step,
            value_per_step,
            log_total,
            weighted,
            att_cols,
            middle,
            inv_two,
            gain_two,
            normed_two,
            gate_pre,
            up_proj,
            activated,
        ) = stored[layer_at]
        grad_low = gradient.astype(jnp.bfloat16)
        down_grads[layer_at] = contract_rows(activated, grad_low)
        dact = contract_cols(grad_low, down_weight[layer_at])
        sigmoid_gate = jax.nn.sigmoid(gate_pre)
        dgate = (dact * up_proj * sigmoid_gate * (1.0 + gate_pre * (1.0 - sigmoid_gate))).astype(
            jnp.bfloat16
        )
        dup_proj = (dact * gate_pre * sigmoid_gate).astype(jnp.bfloat16)
        gate_up_grads[layer_at] = jnp.stack(
            [contract_rows(normed_two, dgate), contract_rows(normed_two, dup_proj)]
        )
        dnormed_two = contract_cols(dgate, gate_up_weight[layer_at, 0]) + contract_cols(
            dup_proj, gate_up_weight[layer_at, 1]
        )
        dnormed_two = width_sum(dnormed_two)
        gain_two_grads[layer_at], dmiddle = norm_backward(dnormed_two, middle, inv_two, gain_two)
        grad_mid = gradient + dmiddle
        mid_low = grad_mid.astype(jnp.bfloat16)
        out_grads[layer_at] = contract_rows(att_cols, mid_low)
        datt_cols = contract_cols(mid_low, out_weight[layer_at]).astype(jnp.bfloat16)
        attention_gradient = lax.all_to_all(
            datt_cols.reshape(blocks_dev, wa_count, sub_rows, col_width),
            "wa",
            split_axis=1,
            concat_axis=3,
            tiled=True,
        )
        gradient_quad = attention_gradient.reshape(
            local_rows, KEY_VALUE_HEADS, head_cluster, HEAD_SIZE
        )
        dquery, key_gradients, dvalues = attend_backward(
            query_quad,
            gradient_quad,
            weighted,
            key_per_step,
            value_per_step,
            key_pos,
            own_pos,
            log_total,
            score_scale,
        )
        key_gradients = key_gradients.reshape(ctx_count * wa_count, local_rows, key_value_width)
        dvalues = dvalues.reshape(ctx_count * wa_count, local_rows, key_value_width)
        key_gradients, dvalues = (
            lax.psum_scatter(key_gradients, ("ctx", "wa"), scatter_dimension=0, tiled=True),
            lax.psum_scatter(dvalues, ("ctx", "wa"), scatter_dimension=0, tiled=True),
        )
        dquery_own = apply_rotary(
            dquery.reshape(local_rows, QUERY_HEADS, HEAD_SIZE), local_cosine, -local_sine
        ).reshape(local_rows, hidden_width)
        local_key_gradient = apply_rotary(
            key_gradients.reshape(local_rows, KEY_VALUE_HEADS, HEAD_SIZE), local_cosine, -local_sine
        ).reshape(local_rows, key_value_width)
        dqkv_own = jnp.concatenate(
            [dquery_own, local_key_gradient, dvalues.reshape(local_rows, key_value_width)], axis=-1
        ).astype(jnp.bfloat16)
        dqkv = lax.all_gather(
            dqkv_own.reshape(blocks_dev, 1, sub_rows, -1), "wa", axis=1, tiled=True
        )
        dqkv = dqkv.reshape(row_count, -1)
        qkv_grads[layer_at] = contract_rows(normed_cols, dqkv)
        dnormed_cols = contract_cols(dqkv, qkv_weight[layer_at])
        dnormed = lax.all_gather(
            dnormed_cols.astype(jnp.bfloat16), "wa", axis=1, tiled=True
        ).astype(dnormed_cols.dtype)
        gain_one_grads[layer_at], dinput = norm_backward(dnormed, layer_input, inv_one, gain_one)
        gradient = grad_mid + dinput
    summed = (
        lax.psum(jnp.stack(gain_one_grads).astype(jnp.bfloat16), "ctx").astype(jnp.float32),
        lax.psum(jnp.stack(qkv_grads).astype(jnp.bfloat16), "ctx").astype(jnp.float32),
        lax.psum(jnp.stack(out_grads).astype(jnp.bfloat16), "ctx").astype(jnp.float32),
        lax.psum(jnp.stack(gain_two_grads).astype(jnp.bfloat16), "ctx").astype(jnp.float32),
        lax.psum(jnp.stack(gate_up_grads).astype(jnp.bfloat16), "ctx").astype(jnp.float32),
        lax.psum(jnp.stack(down_grads).astype(jnp.bfloat16), "ctx").astype(jnp.float32),
    )
    return (residual, gradient, summed[0], summed[1], summed[2], summed[3], summed[4], summed[5])


def solution(mesh):
    placed = (
        P("ctx", None),
        P(),
        P(),
        P(None, "wa", None),
        P(None, "wa", None),
        P(),
        P(None, None, None, "wa"),
        P(None, "wa", None),
        P("ctx", None),
    )
    return jax.shard_map(
        per_device,
        mesh=mesh,
        in_specs=placed,
        out_specs=(
            P("ctx", None),
            P("ctx", None),
            P(),
            P(None, "wa", None),
            P(None, "wa", None),
            P(),
            P(None, None, None, "wa"),
            P(None, "wa", None),
        ),
        check_vma=False,
    )
```

profile of v0, /device:TPU:0, one launch (start us, length us, event | category | flops | bytes accessed | tf_op | source)
XLA Modules:
  0.0 1768.1 jit_solution(6625103377135172208)
XLA Ops:
  12.8 54.8 %all-reduce.22.cloned.1.call-done = bf16[4,4,32,960]{3,2,1,0:T(8,128)(2,1)} async-done(((bf16[4,4,32,960]{3,2,1,0:T(8,128)(2,1)}), bf16[4,4,32,960]{3,2,1,0:T(8,128)(2,1)}) %all-reduce.22.cloned.1.call-update) | async-done | bytes 983056
  74.4 53.1 %all-gather.11.cloned.1.call-done = bf16[4096,192]{1,0:T(8,128)(2,1)} async-done(((bf16[128,192]{1,0:T(8,128)(2,1)}), bf16[4096,192]{1,0:T(8,128)(2,1)}) %all-gather.11.cloned.1.call-update) | async-done | bytes 1572880 | tf_op jit(solution)/shard_map/all_gather | solution.py:231
  135.7 49.1 %all-gather.7.cloned.1.call-done = bf16[32,128,192]{1,2,0:T(8,128)(2,1)} async-done(((bf16[1,128,192]{1,2,0:T(8,128)(2,1)}), bf16[32,128,192]{1,2,0:T(8,128)(2,1)}) %all-gather.7.cloned.1.call-update) | async-done | bytes 1572880 | tf_op jit(solution)/shard_map/all_gather | solution.py:230
  192.2 36.5 %while.78 = (s32[]{:T(128)}, f32[3,3,128]{2,1,0:T(4,128)S(1)}, f32[3,3,128]{2,1,0:T(4,128)S(1)}, s32[4,1024]{1,0:T(4,128)}, bf16[4,1024,3,64]{1,3,2,0:T(8,128)(2...) while((s32[]{:T(128)}, f32[3,3,128]{2,1,0:T(4,128)S(1)}, ...), condition=%wide.region_5.6_spmd.clone, body=%wide.region_2.5_spmd.clone.sunk | while | flops 159389440 | bytes 10445448 | solution.py:85
  228.7 16.9 while.79
  258.4 43.1 %all-reduce.14.cloned.1.call-done = bf16[512,576]{0,1:T(8,128)(2,1)} async-done(((bf16[512,576]{0,1:T(8,128)(2,1)}), bf16[512,576]{0,1:T(8,128)(2,1)}) %all-reduce.14.cloned.1.call-update) | async-done | bytes 589840 | tf_op jit(solution)/shard_map/psum | solution.py:51
  307.0 46.1 %all-reduce.16.cloned.1.call-done = bf16[512,576]{0,1:T(8,128)(2,1)} async-done(((bf16[512,576]{0,1:T(8,128)(2,1)}), bf16[512,576]{0,1:T(8,128)(2,1)}) %all-reduce.16.cloned.1.call-update) | async-done | bytes 589840 | tf_op jit(solution)/shard_map/psum | solution.py:51
  357.4 52.7 %all-reduce.24.cloned.1.call-done = bf16[4,4,32,960]{3,2,1,0:T(8,128)(2,1)} async-done(((bf16[4,4,32,960]{3,2,1,0:T(8,128)(2,1)}), bf16[4,4,32,960]{3,2,1,0:T(8,128)(2,1)}) %all-reduce.24.cloned.1.call-update) | async-done | bytes 983056
  413.7 56.2 %all-gather.13.cloned.1.call-done = bf16[4096,192]{1,0:T(8,128)(2,1)} async-done(((bf16[128,192]{1,0:T(8,128)(2,1)}), bf16[4096,192]{1,0:T(8,128)(2,1)}) %all-gather.13.cloned.1.call-update) | async-done | bytes 1572880 | tf_op jit(solution)/shard_map/all_gather | solution.py:231
  480.7 46.6 %all-gather.9.cloned.1.call-done = bf16[32,128,192]{1,2,0:T(8,128)(2,1)} async-done(((bf16[1,128,192]{1,2,0:T(8,128)(2,1)}), bf16[32,128,192]{1,2,0:T(8,128)(2,1)}) %all-gather.9.cloned.1.call-update) | async-done | bytes 1572880 | tf_op jit(solution)/shard_map/all_gather | solution.py:230
  537.4 36.1 %while.80 = (s32[]{:T(128)}, f32[3,3,128]{2,1,0:T(4,128)S(1)}, f32[3,3,128]{2,1,0:T(4,128)S(1)}, s32[4,1024]{1,0:T(4,128)}, bf16[4,1024,3,64]{1,3,2,0:T(8,128)(2...) while((s32[]{:T(128)}, f32[3,3,128]{2,1,0:T(4,128)S(1)}, ...), condition=%wide.region_16.17_spmd.clone, body=%wide.region_13.16_spmd.clone.sunk | while | flops 159389440 | bytes 10445448 | solution.py:85
  573.5 16.9 while.81
  603.4 44.2 %all-reduce.18.cloned.1.call-done = bf16[512,576]{0,1:T(8,128)(2,1)} async-done(((bf16[512,576]{0,1:T(8,128)(2,1)}), bf16[512,576]{0,1:T(8,128)(2,1)}) %all-reduce.18.cloned.1.call-update) | async-done | bytes 589840 | tf_op jit(solution)/shard_map/psum | solution.py:51
  656.6 46.2 %all-reduce.20.cloned.1.call-done = bf16[512,576]{0,1:T(8,128)(2,1)} async-done(((bf16[512,576]{0,1:T(8,128)(2,1)}), bf16[512,576]{0,1:T(8,128)(2,1)}) %all-reduce.20.cloned.1.call-update) | async-done | bytes 589840 | tf_op jit(solution)/shard_map/psum | solution.py:51
  724.1 191.8 %while.82 = (s32[]{:T(128)}, f32[128,3,3,64]{0,3,2,1:T(8,128)S(1)}, f32[4,1024,3,64]{1,0,3,2:T(4,128)}, f32[4,1024,3,64]{1,0,3,2:T(4,128)}, bf16[4,1024,3,64]{1,...) while((s32[]{:T(128)}, f32[128,3,3,64]{0,3,2,1:T(8,128)S(1)}, ...), condition=%wide.region_25.26_spmd.clone, body=%wide.region_24.25_spmd.clone.sunk | while | flops 768229504 | bytes 33538864 | solution.py:143
  756.8 15.3 dynamic_update_slice.22
  804.8 15.3 dynamic_update_slice.22
  940.5 87.4 %reduce-scatter.7.cloned.1.call-done = f32[1,128,192]{1,2,0:T(8,128)} async-done(((f32[32,128,192]{1,2,0:T(8,128)}), f32[1,128,192]{1,2,0:T(8,128)}) %reduce-scatter.7.cloned.1.call-update) | async-done | bytes 98320 | tf_op jit(solution)/shard_map/reduce_scatter | solution.py:357
  1029.1 104.7 %reduce-scatter.9.cloned.1.call-done = f32[1,128,192]{1,2,0:T(8,128)} async-done(((f32[32,128,192]{1,2,0:T(8,128)}), f32[1,128,192]{1,2,0:T(8,128)}) %reduce-scatter.9.cloned.1.call-update) | async-done | bytes 98320 | tf_op jit(solution)/shard_map/reduce_scatter | solution.py:358
  1166.0 53.0 %all-reduce.28.cloned.1.call-done = (bf16[512,576]{0,1:T(8,128)(2,1)}, bf16[512,576]{0,1:T(8,128)(2,1)}) async-done(((bf16[512,576]{0,1:T(8,128)(2,1)}, bf16[512,576]{0,1:T(8,128)(2,1)}), (bf16[512,576]{0,1:T(8,128)(2,1)}, bf16[512,576]{0,1:T(8,128)(2,1)})) %all-reduce.28.cloned.1.call-update) | async-done | bytes 1179664 | tf_op jit(solution)/shard_map/psum | solution.py:51
  1240.0 191.5 %while.83 = (s32[]{:T(128)}, f32[128,3,3,64]{0,3,2,1:T(8,128)S(1)}, f32[4,1024,3,64]{1,0,3,2:T(4,128)}, f32[4,1024,3,64]{1,0,3,2:T(4,128)}, bf16[4,1024,3,64]{1,...) while((s32[]{:T(128)}, f32[128,3,3,64]{0,3,2,1:T(8,128)S(1)}, ...), condition=%wide.region_32.33_spmd.clone, body=%wide.region_31.32_spmd.clone.sunk | while | flops 768229504 | bytes 32488696 | solution.py:143
  1466.1 77.3 %reduce-scatter.11.cloned.1.call-done = f32[1,128,192]{1,2,0:T(8,128)} async-done(((f32[32,128,192]{1,2,0:T(8,128)}), f32[1,128,192]{1,2,0:T(8,128)}) %reduce-scatter.11.cloned.1.call-update) | async-done | bytes 98320 | tf_op jit(solution)/shard_map/reduce_scatter | solution.py:357
  1544.6 105.6 %reduce-scatter.13.cloned.1.call-done = f32[1,128,192]{1,2,0:T(8,128)} async-done(((f32[32,128,192]{1,2,0:T(8,128)}), f32[1,128,192]{1,2,0:T(8,128)}) %reduce-scatter.13.cloned.1.call-update) | async-done | bytes 98320 | tf_op jit(solution)/shard_map/reduce_scatter | solution.py:358
  1698.6 55.2 %all-reduce.26.cloned.1.call-done = (bf16[2,144,960]{2,1,0:T(8,128)(2,1)}, bf16[2,144,576]{2,1,0:T(8,128)(2,1)}, bf16[2,2,576,384]{3,2,1,0:T(8,128)(2,1)}, bf16[2,384,576]{1,2,0:T(8,128)(2,1)}) async-done(((bf16[2,144,960]{2,1,0:T(8,128)(2,1)}, bf16[2,144,576]{2,1,0:T(8,128)(2,1)}, bf16[2,2,576,384]{3,2,1,0:T(8,128)(2,1)}, bf16[2,384,576]{1,2,0:T(8,128)(2,1)}), (bf16[2,144,960]{2,1,0:T(8,128)(2,1)}, ...) | async-done | bytes 3538960 | tf_op jit(solution)/shard_map/psum | solution.py:382
  (696 shorter events, 745.4 us)
Async XLA Ops:
  7.2 60.4 %all-reduce.22.cloned.1.call-start = ((), (), s32[]{:S(2)}) async-start(), calls=%async_computation.20 | async-start | bytes 2097152
  9.8 297.1 %copy-start.79 = (f32[576]{0:T(1024)}, f32[576]{0:T(1024)S(1)}, u32[]{:S(2)}) copy-start(f32[576]{0:T(1024)S(1)} %get-tuple-element.694) | copy-start | bytes 6916
  10.6 58.6 %copy-start.50 = (bf16[512,144]{0,1:T(8,128)(2,1)}, bf16[512,144]{0,1:T(8,128)(2,1)S(1)}, u32[]{:S(2)}) copy-start(bf16[512,144]{0,1:T(8,128)(2,1)S(1)} %fusion.195) | copy-start | bytes 442372
  10.8 59.2 %copy-start.96 = (s32[16]{0:T(128)S(1)}, s32[16]{0:T(128)}, u32[]{:S(2)}) copy-start(s32[16]{0:T(128)} %param.22) | copy-start | bytes 196
  12.2 115.3 %all-gather.11.cloned.1.call-start = ((), (), s32[]{:S(2)}) async-start(), calls=%async_computation.18 | async-start | bytes 2162688 | tf_op jit(solution)/shard_map/all_gather | solution.py:231
  69.9 114.9 %all-gather.7.cloned.1.call-start = ((), (), s32[]{:S(2)}) async-start(), calls=%async_computation.8 | async-start | bytes 1622016 | tf_op jit(solution)/shard_map/all_gather | solution.py:230
  73.1 228.4 %all-reduce.14.cloned.1.call-start = ((), (), s32[]{:S(2)}) async-start(), calls=%async_computation.9 | async-start | bytes 1179648 | tf_op jit(solution)/shard_map/psum | solution.py:51
  257.2 95.8 %all-reduce.16.cloned.1.call-start = ((), (), s32[]{:S(2)}) async-start(), calls=%async_computation.10 | async-start | bytes 1179648 | tf_op jit(solution)/shard_map/psum | solution.py:51
  306.8 103.2 %all-reduce.24.cloned.1.call-start = ((), (), s32[]{:S(2)}) async-start(), calls=%async_computation.21 | async-start | bytes 2097152
  354.4 293.2 %copy-start.3 = (f32[512,576]{0,1:T(8,128)}, f32[512,576]{0,1:T(8,128)S(1)}, u32[]{:S(2)}) copy-start(f32[512,576]{0,1:T(8,128)S(1)} %get-tuple-element.815) | copy-start | bytes 3538948
  354.7 57.0 %copy-start.52 = (bf16[512,144]{0,1:T(8,128)(2,1)}, bf16[512,144]{0,1:T(8,128)(2,1)S(1)}, u32[]{:S(2)}) copy-start(bf16[512,144]{0,1:T(8,128)(2,1)S(1)} %fusion.194) | copy-start | bytes 442372
  357.4 112.6 %all-gather.13.cloned.1.call-start = ((), (), s32[]{:S(2)}) async-start(), calls=%async_computation.19 | async-start | bytes 2162688 | tf_op jit(solution)/shard_map/all_gather | solution.py:231
  412.4 114.9 %all-gather.9.cloned.1.call-start = ((), (), s32[]{:S(2)}) async-start(), calls=%async_computation.11 | async-start | bytes 1622016 | tf_op jit(solution)/shard_map/all_gather | solution.py:230
  413.4 234.2 %all-reduce.18.cloned.1.call-start = ((), (), s32[]{:S(2)}) async-start(), calls=%async_computation.12 | async-start | bytes 1179648 | tf_op jit(solution)/shard_map/psum | solution.py:51
  603.3 99.5 %all-reduce.20.cloned.1.call-start = ((), (), s32[]{:S(2)}) async-start(), calls=%async_computation.13 | async-start | bytes 1179648 | tf_op jit(solution)/shard_map/psum | solution.py:51
  707.7 8.8 all-to-all-start.2
  711.1 316.8 %reduce-scatter.7.cloned.1.call-start = ((), (), s32[]{:S(2)}) async-start(), calls=%async_computation.14 | async-start | bytes 3244032 | tf_op jit(solution)/shard_map/reduce_scatter | solution.py:357
  926.4 207.4 %reduce-scatter.9.cloned.1.call-start = ((), (), s32[]{:S(2)}) async-start(), calls=%async_computation.15 | async-start | bytes 3244032 | tf_op jit(solution)/shard_map/reduce_scatter | solution.py:358
  937.2 281.7 %all-reduce.28.cloned.1.call-start = ((), (), s32[]{:S(2)}) async-start(), calls=%async_computation.23 | async-start | bytes 2359296 | tf_op jit(solution)/shard_map/psum | solution.py:51
  1160.9 60.4 %copy-start.12 = (f32[512,576]{0,1:T(8,128)}, f32[512,576]{0,1:T(8,128)S(1)}, u32[]{:S(2)}) copy-start(f32[512,576]{0,1:T(8,128)S(1)} %fusion.144) | copy-start | bytes 3538948
  1223.9 9.0 all-to-all-start.3
  1227.3 316.1 %reduce-scatter.11.cloned.1.call-start = ((), (), s32[]{:S(2)}) async-start(), calls=%async_computation.16 | async-start | bytes 3244032 | tf_op jit(solution)/shard_map/reduce_scatter | solution.py:357
  1441.9 208.2 %reduce-scatter.13.cloned.1.call-start = ((), (), s32[]{:S(2)}) async-start(), calls=%async_computation.17 | async-start | bytes 3244032 | tf_op jit(solution)/shard_map/reduce_scatter | solution.py:358
  1452.7 301.1 %all-reduce.26.cloned.1.call-start = ((), (), s32[]{:S(2)}) async-start(), calls=%async_computation.22 | async-start | bytes 7225344 | tf_op jit(solution)/shard_map/psum | solution.py:382
  (113 other events, 1041.8 us)
Sparse Core Ops, SparseCore 0:
  12.3 55.2 all-reduce.21
  71.0 56.3 all-gather.10
  130.9 53.8 all-gather.6
  257.4 44.0 all-reduce.13
  307.0 46.0 all-reduce.15
  357.5 52.5 all-reduce.23
  413.5 56.3 all-gather.12
  473.4 53.8 all-gather.8
  603.4 44.1 all-reduce.17
  656.7 46.0 all-reduce.19
  926.5 101.3 reduce-scatter.6
  1033.2 100.5 reduce-scatter.8
  1166.1 52.7 all-reduce.27
  1442.1 101.3 reduce-scatter.10
  1549.6 100.4 reduce-scatter.12
  1666.7 87.0 all-reduce.25
where the time goes:
time: 1790 us; the launch traced here: 1770 us
  waiting for transfers between devices  986 us (55%)
  local copies, waits for them, and re-layouts  402 us (22%)
  matrix products  190 us (11%)
  other arithmetic  86.2 us (5%)
  blocking collectives  78.6 us (4%)
    dynamic_update_slice x32, local copies, waits for them, and re-layouts, attend_backward(): lax.scan(second_pass, jnp.zeros(query_quad.shape, jnp.float32), (key_per_...  257 us
    psum x5, waiting for transfers between devices, width_sum(): lax.psum(partial_value.astype(jnp.bfloat16), 'wa').astype(jnp.float32)  233 us
    reduce_scatter x2, waiting for transfers between devices, per_device(): lax.psum_scatter(dvalues, ('ctx', 'wa'), scatter_dimension=0, tiled=True)  210 us
    reduce_scatter x2, waiting for transfers between devices, per_device(): lax.psum_scatter(key_gradients, ('ctx', 'wa'), scatter_dimension=0, tiled...  165 us
    all_gather x2, waiting for transfers between devices, per_device(): lax.all_gather(value_matrix_rows, ('ctx', 'wa'), axis=0, tiled=True)  109 us
    unnamed x18, waiting for transfers between devices  108 us
    all_gather x2, waiting for transfers between devices, per_device(): lax.all_gather(key_matrix_rows, ('ctx', 'wa'), axis=0, tiled=True)  95.7 us
    dot_general x16, matrix products, score_block(): jnp.einsum('qgrd,kgd->grqk', query_quad, key_blk, preferred_element_type=...  63.8 us
  transfers between devices with their start and end apart: 18, of which 18 were waited for; matrix products, arithmetic and copies ran while one was open for 4% of the time, Pallas kernels for 0%

commit v1 on v0

v1 whole, which is shorter than its diff:
```python
import functools

import jax
import jax.numpy as jnp
from jax import lax
from jax.experimental import pallas as pl
from jax.experimental.pallas import tpu as pltpu
from jax.sharding import PartitionSpec as P

QUERY_HEADS = 9
KEY_VALUE_HEADS = 3
HEAD_SIZE = 64
BLK = 128
LAYERS = 2


EPSILON = 1e-05
KEY_CHUNK = 512
VMEM_BYTES = 50 * 1024 * 1024


def rotation(token_pos, head_width):
    half_width = head_width // 2
    inv_freq = jnp.power(
        jnp.float32(100000.0), -2.0 * jnp.arange(half_width, dtype=jnp.float32) / head_width
    )
    angles = token_pos.astype(jnp.float32)[..., None] * inv_freq
    return (jnp.cos(angles), jnp.sin(angles))


def apply_rotary(vectors, cosine, sine):
    half_width = vectors.shape[-1] // 2
    first_half = vectors[..., :half_width]
    second_half = vectors[..., half_width:]
    cosine = cosine[..., None, :]
    sine = sine[..., None, :]
    return jnp.concatenate(
        [first_half * cosine - second_half * sine, second_half * cosine + first_half * sine],
        axis=-1,
    )


def contract_rows(left, right):
    return lax.dot_general(
        left, right, (((0,), (0,)), ((), ())), preferred_element_type=jnp.float32
    )


def contract_cols(left, right):
    return lax.dot_general(
        left, right, (((1,), (1,)), ((), ())), preferred_element_type=jnp.float32
    )


def norm_backward(grad_normed, source, inv_root, gain_row):
    gain_grad = jnp.sum(grad_normed * source * inv_root, axis=0)
    weighted = grad_normed * gain_row
    back = inv_root * (
        weighted
        - source * inv_root * inv_root * jnp.mean(weighted * source, axis=-1, keepdims=True)
    )
    return (gain_grad, back)


def group_of(kind):
    ctx_at = lax.axis_index("ctx")
    if kind == "wa":
        return lax.axis_size("wa"), lax.axis_index("wa"), lambda p: {"wa": p}
    core = lax.rem(ctx_at, 2)
    if kind == "core":
        return 2, core, lambda p: {"ctx": ctx_at - core + p}
    return lax.axis_size("ctx") // 2, lax.div(ctx_at, 2), lambda p: {"ctx": 2 * p + core}


def exchange_kernel(kind, gather, x_ref, out_ref, own_sem, send_sem, recv_sem):
    count, me, device = group_of(kind)
    own = pltpu.make_async_copy(x_ref if gather else x_ref.at[me], out_ref.at[me], own_sem)
    own.start()
    barrier = pltpu.get_barrier_semaphore()
    for step in range(1, count):
        pl.semaphore_signal(
            barrier,
            inc=1,
            device_id=device(lax.rem(me + step, count)),
            device_id_type=pl.DeviceIdType.MESH,
        )
    pl.semaphore_wait(barrier, count - 1)
    copies = []
    for step in range(1, count):
        peer = lax.rem(me + step, count)
        copy = pltpu.make_async_remote_copy(
            src_ref=x_ref if gather else x_ref.at[peer],
            dst_ref=out_ref.at[me],
            send_sem=send_sem.at[step - 1],
            recv_sem=recv_sem.at[step - 1],
            device_id=device(peer),
            device_id_type=pl.DeviceIdType.MESH,
        )
        copy.start()
        copies.append(copy)
    own.wait()
    for copy in copies:
        copy.wait()


class Links:
    def __init__(self):
        self.ids = {}

    def run(self, kind, gather, x):
        count = group_of(kind)[0]
        out_shape = (count,) + x.shape if gather else x.shape
        key = (kind, gather, x.shape)
        collective = self.ids.setdefault(key, len(self.ids))
        return pl.pallas_call(
            functools.partial(exchange_kernel, kind, gather),
            out_shape=jax.ShapeDtypeStruct(out_shape, x.dtype),
            in_specs=[pl.BlockSpec(memory_space=pl.ANY)],
            out_specs=pl.BlockSpec(memory_space=pl.ANY),
            scratch_shapes=[
                pltpu.SemaphoreType.DMA,
                pltpu.SemaphoreType.DMA((count - 1,)),
                pltpu.SemaphoreType.DMA((count - 1,)),
            ],
            compiler_params=pltpu.CompilerParams(
                collective_id=collective, has_side_effects=True
            ),
        )(x)

    def gather(self, kind, x):
        return self.run(kind, True, x)

    def reduce(self, kind, x):
        return jnp.sum(self.run(kind, False, x.astype(jnp.bfloat16)).astype(jnp.float32), axis=0)


def dot_of(left, right, left_dim, right_dim):
    return lax.dot_general(
        left,
        right,
        (((left_dim,), (right_dim,)), ((), ())),
        preferred_element_type=jnp.float32,
    )


def attend_forward_kernel(q_ref, kv_ref, kpos_ref, qpos_ref, out_ref, lse_ref):
    key_count = kv_ref.shape[0]
    value_at = KEY_VALUE_HEADS * HEAD_SIZE
    query_count = q_ref.shape[1]
    query_pos = qpos_ref[...]
    for head in range(KEY_VALUE_HEADS):
        lo = head * HEAD_SIZE
        query = q_ref[head]

        def body(step, carry):
            top, total, acc = carry
            rows = pl.ds(pl.multiple_of(step * KEY_CHUNK, KEY_CHUNK), KEY_CHUNK)
            key = kv_ref[rows, lo : lo + HEAD_SIZE]
            value = kv_ref[rows, value_at + lo : value_at + lo + HEAD_SIZE]
            live = kpos_ref[rows, :] <= query_pos
            score = jnp.where(live, dot_of(key, query, 1, 1), -1e30)
            new_top = jnp.maximum(top, jnp.max(score, axis=0, keepdims=True))
            prob = jnp.exp(score - new_top)
            keep = jnp.exp(top - new_top)
            total = total * keep + jnp.sum(prob, axis=0, keepdims=True)
            acc = acc * keep + dot_of(value, prob.astype(jnp.bfloat16), 0, 0)
            return new_top, total, acc

        top, total, acc = lax.fori_loop(
            0,
            key_count // KEY_CHUNK,
            body,
            (
                jnp.full((1, query_count), -1e30, jnp.float32),
                jnp.zeros((1, query_count), jnp.float32),
                jnp.zeros((HEAD_SIZE, query_count), jnp.float32),
            ),
        )
        out_ref[head] = acc / total
        lse_ref[head] = top + jnp.log(total)


def attend_backward_kernel(
    q_ref, do_ref, kv_ref, kpos_ref, qpos_ref, lse_ref, delta_ref, dq_ref, dkv_ref
):
    key_count = kv_ref.shape[0]
    value_at = KEY_VALUE_HEADS * HEAD_SIZE
    query_count = q_ref.shape[1]
    query_pos = qpos_ref[...]
    for head in range(KEY_VALUE_HEADS):
        lo = head * HEAD_SIZE
        query = q_ref[head]
        grad = do_ref[head]
        lse = lse_ref[head]
        delta = delta_ref[head]

        def body(step, dquery):
            rows = pl.ds(pl.multiple_of(step * KEY_CHUNK, KEY_CHUNK), KEY_CHUNK)
            key = kv_ref[rows, lo : lo + HEAD_SIZE]
            value = kv_ref[rows, value_at + lo : value_at + lo + HEAD_SIZE]
            live = kpos_ref[rows, :] <= query_pos
            score = jnp.where(live, dot_of(key, query, 1, 1), -1e30)
            prob = jnp.exp(score - lse)
            dscore = (prob * (dot_of(value, grad, 1, 1) - delta)).astype(jnp.bfloat16)
            dkv_ref[rows, lo : lo + HEAD_SIZE] = dot_of(dscore, query, 1, 0).astype(jnp.bfloat16)
            dkv_ref[rows, value_at + lo : value_at + lo + HEAD_SIZE] = dot_of(
                prob.astype(jnp.bfloat16), grad, 1, 0
            ).astype(jnp.bfloat16)
            return dquery + dot_of(key, dscore, 0, 0)

        dq_ref[head] = lax.fori_loop(
            0,
            key_count // KEY_CHUNK,
            body,
            jnp.zeros((HEAD_SIZE, query_count), jnp.float32),
        )


def local_call(kernel, out_shapes, *arrays):
    vmem = pl.BlockSpec(memory_space=pltpu.VMEM)
    return pl.pallas_call(
        kernel,
        out_shape=[jax.ShapeDtypeStruct(s, t) for s, t in out_shapes],
        in_specs=[vmem] * len(arrays),
        out_specs=[vmem] * len(out_shapes),
        compiler_params=pltpu.CompilerParams(vmem_limit_bytes=VMEM_BYTES),
    )(*arrays)


def heads_in(rows):
    count = rows.shape[0]
    split = rows.reshape(count, QUERY_HEADS, HEAD_SIZE).transpose(1, 0, 2)
    return split.reshape(KEY_VALUE_HEADS, -1, HEAD_SIZE)


def heads_out(columns, count):
    split = columns.reshape(KEY_VALUE_HEADS, HEAD_SIZE, -1, count)
    return split.transpose(3, 0, 2, 1).reshape(count, QUERY_HEADS * HEAD_SIZE)


def per_device(
    hidden_in,
    pair_table,
    norm1_gain,
    qkv_weight,
    out_weight,
    norm2_gain,
    gate_up_weight,
    down_weight,
    out_grad,
):
    ctx_count = lax.axis_size("ctx")
    wa_count = lax.axis_size("wa")
    ctx_at = lax.axis_index("ctx")
    wa_at = lax.axis_index("wa")
    links = Links()
    row_count, width = hidden_in.shape
    pairs_total = pair_table.shape[0]
    own_rows = row_count // wa_count
    kv_width = KEY_VALUE_HEADS * HEAD_SIZE
    score_scale = HEAD_SIZE ** (-0.5)
    key_count = ctx_count * row_count
    z_count = ctx_count // 2
    low = jnp.bfloat16
    full = jnp.float32
    seq_blocks = jnp.stack([pair_table, 2 * pairs_total - 1 - pair_table], axis=1).reshape(-1)
    all_pos = (seq_blocks[:, None] * BLK + jnp.arange(BLK, dtype=jnp.int32)[None, :]).reshape(-1)
    own_pos = lax.dynamic_slice_in_dim(
        all_pos, ctx_at * row_count + wa_at * own_rows, own_rows, 0
    )
    query_pos = jnp.tile(own_pos, QUERY_HEADS // KEY_VALUE_HEADS)[None, :]
    key_pos = all_pos.reshape(z_count, 2, wa_count, own_rows).transpose(1, 2, 0, 3).reshape(-1, 1)
    cosine, sine = rotation(own_pos, HEAD_SIZE)

    def own(rows):
        return lax.dynamic_slice_in_dim(rows, wa_at * own_rows, own_rows, 0)

    def gather_rows(rows):
        return links.gather("wa", rows.astype(low)).reshape(row_count, width)

    def reduce_rows(partial_value):
        return links.reduce("wa", partial_value.reshape(wa_count, own_rows, width))

    def rope(rows, heads, sine_of):
        return apply_rotary(rows.reshape(own_rows, heads, HEAD_SIZE), cosine, sine_of).reshape(
            own_rows, heads * HEAD_SIZE
        )

    qkv_full = [links.gather("wa", qkv_weight[0]).reshape(width, -1)]
    qkv_full += [
        lax.all_gather(qkv_weight[layer], "wa", axis=0, tiled=True) for layer in range(1, LAYERS)
    ]
    out_full = [lax.all_gather(out_weight[layer], "wa", axis=0, tiled=True) for layer in range(LAYERS)]
    residual = own(hidden_in).astype(full)
    stored = []
    for layer in range(LAYERS):
        gain_one = norm1_gain[layer].astype(full)
        inv_one = lax.rsqrt(jnp.mean(residual * residual, axis=-1, keepdims=True) + EPSILON)
        normed = (residual * inv_one * gain_one).astype(low)
        qkv = jnp.dot(normed, qkv_full[layer], preferred_element_type=full)
        query = heads_in((rope(qkv[:, :width], QUERY_HEADS, sine).astype(low) * score_scale).astype(low))
        key_value = jnp.concatenate(
            [
                rope(qkv[:, width : width + kv_width], KEY_VALUE_HEADS, sine).astype(low),
                qkv[:, width + kv_width :].astype(low),
            ],
            axis=1,
        )
        key_value = links.gather("z", key_value).reshape(-1, 2 * kv_width)
        key_value = links.gather("wa", key_value).reshape(-1, 2 * kv_width)
        key_value = links.gather("core", key_value).reshape(key_count, 2 * kv_width)
        columns = query.shape[1]
        attended, log_total = local_call(
            attend_forward_kernel,
            [
                ((KEY_VALUE_HEADS, HEAD_SIZE, columns), full),
                ((KEY_VALUE_HEADS, 1, columns), full),
            ],
            query,
            key_value,
            key_pos,
            query_pos,
        )
        weighted = heads_out(attended, own_rows)
        att = weighted.astype(low)
        middle = residual + jnp.dot(att, out_full[layer], preferred_element_type=full)
        gain_two = norm2_gain[layer].astype(full)
        inv_two = lax.rsqrt(jnp.mean(middle * middle, axis=-1, keepdims=True) + EPSILON)
        normed_two = gather_rows((middle * inv_two * gain_two).astype(low))
        gate = jnp.dot(normed_two, gate_up_weight[layer, 0], preferred_element_type=full)
        up = jnp.dot(normed_two, gate_up_weight[layer, 1], preferred_element_type=full)
        activated = (jax.nn.silu(gate) * up).astype(low)
        output_rows = middle + reduce_rows(
            jnp.dot(activated, down_weight[layer], preferred_element_type=full)
        )
        stored.append(
            (residual, inv_one, gain_one, normed, query, key_value, log_total, weighted, att)
            + (middle, inv_two, gain_two, normed_two, gate, up, activated)
        )
        residual = output_rows
    hidden_out = gather_rows(residual).astype(full)
    gradient = own(out_grad).astype(full)
    grad_low = out_grad
    row_grads = [None] * LAYERS
    gate_up_grads = [None] * LAYERS
    down_grads = [None] * LAYERS
    for layer in reversed(range(LAYERS)):
        (
            (layer_input, inv_one, gain_one, normed, query, key_value, log_total, weighted, att)
        ) = stored[layer][:9]
        middle, inv_two, gain_two, normed_two, gate, up, activated = stored[layer][9:]
        down_grads[layer] = contract_rows(activated, grad_low)
        dact = contract_cols(grad_low, down_weight[layer])
        sig = jax.nn.sigmoid(gate)
        dgate = (dact * up * sig * (1.0 + gate * (1.0 - sig))).astype(low)
        dup = (dact * gate * sig).astype(low)
        gate_up_grads[layer] = jnp.stack(
            [contract_rows(normed_two, dgate), contract_rows(normed_two, dup)]
        )
        dnormed_two = reduce_rows(
            contract_cols(dgate, gate_up_weight[layer, 0])
            + contract_cols(dup, gate_up_weight[layer, 1])
        )
        gain_two_grad, dmiddle = norm_backward(dnormed_two, middle, inv_two, gain_two)
        grad_mid = gradient + dmiddle
        mid_low = grad_mid.astype(low)
        out_part = contract_rows(att, mid_low)
        datt = contract_cols(mid_low, out_full[layer]).astype(low)
        delta = jnp.sum(
            (datt.astype(full) * weighted).reshape(own_rows, QUERY_HEADS, HEAD_SIZE), axis=-1
        )
        delta = delta.T.reshape(KEY_VALUE_HEADS, 1, -1)
        columns = query.shape[1]
        dquery, dkv = local_call(
            attend_backward_kernel,
            [
                ((KEY_VALUE_HEADS, HEAD_SIZE, columns), full),
                ((key_count, 2 * kv_width), low),
            ],
            query,
            heads_in(datt),
            key_value,
            key_pos,
            query_pos,
            log_total,
            delta,
        )
        dkv = links.reduce("core", dkv.reshape(2, -1, 2 * kv_width))
        dkv = links.reduce("wa", dkv.reshape(wa_count, -1, 2 * kv_width))
        dkv = links.reduce("z", dkv.reshape(z_count, -1, 2 * kv_width))
        dqkv = jnp.concatenate(
            [
                rope(heads_out(dquery, own_rows) * score_scale, QUERY_HEADS, -sine),
                rope(dkv[:, :kv_width], KEY_VALUE_HEADS, -sine),
                dkv[:, kv_width:],
            ],
            axis=-1,
        ).astype(low)
        qkv_part = contract_rows(normed, dqkv)
        dnormed = contract_cols(dqkv, qkv_full[layer])
        gain_one_grad, dinput = norm_backward(dnormed, layer_input, inv_one, gain_one)
        gradient = grad_mid + dinput
        if layer > 0:
            grad_low = gather_rows(gradient)
        block = jnp.concatenate([qkv_part, out_part], axis=1).astype(low)
        block = block.reshape(wa_count, -1, block.shape[1])
        gains = jnp.concatenate(
            [gain_one_grad, gain_two_grad, jnp.zeros((block.shape[2] - 2 * width,), full)]
        ).astype(low)
        pad_rows = 16 + (-block.shape[1]) % 16
        gains = jnp.broadcast_to(gains, (wa_count, pad_rows, gains.shape[0]))
        row_grads[layer] = links.reduce("wa", jnp.concatenate([block, gains], axis=1))
    input_grad = gather_rows(gradient).astype(full)
    slab = qkv_weight.shape[1]
    rows_sum, gate_up_sum, down_sum = (
        lax.psum(jnp.stack(part).astype(low), "ctx").astype(full)
        for part in (row_grads, gate_up_grads, down_grads)
    )
    qkv_cols = qkv_weight.shape[2]
    return (
        hidden_out,
        input_grad,
        rows_sum[:, slab, :width],
        rows_sum[:, :slab, :qkv_cols],
        rows_sum[:, :slab, qkv_cols:],
        rows_sum[:, slab, width : 2 * width],
        gate_up_sum,
        down_sum,
    )


def solution(mesh):
    placed = (
        P("ctx", None),
        P(),
        P(),
        P(None, "wa", None),
        P(None, "wa", None),
        P(),
        P(None, None, None, "wa"),
        P(None, "wa", None),
        P("ctx", None),
    )
    return jax.shard_map(
        per_device,
        mesh=mesh,
        in_specs=placed,
        out_specs=(
            P("ctx", None),
            P("ctx", None),
            P(),
            P(None, "wa", None),
            P(None, "wa", None),
            P(),
            P(None, None, None, "wa"),
            P(None, "wa", None),
        ),
        check_vma=False,
    )
```

time: 1790 us -> 780 us (0.44); the launches traced: 1770 us -> 778 us
  waiting for transfers between devices: 986 us -> 64.9 us
  Pallas kernels: 0 us -> 527 us
  local copies, waits for them, and re-layouts: 402 us -> 42.9 us
  matrix products: 190 us -> 45 us
  blocking collectives: 78.6 us -> 27.2 us
  other arithmetic: 86.2 us -> 55.3 us
    pallas_call x0 -> x28, Pallas kernels: none -> 527 us  [the longest x24 451 us: run(): pl.pallas_call(functools.partial(exchange_kernel, kind, gather), out_shap...]
    reduce_scatter x4 -> x0, waiting for transfers between devices: 375 us -> none  [the longest x2 210 us: per_device(): lax.psum_scatter(dvalues, ('ctx', 'wa'), scatter_dimension=0, tiled=True)]
    dynamic_update_slice x32 -> x0, local copies, waits for them, and re-layouts: 257 us -> none  [attend_backward(): lax.scan(second_pass, jnp.zeros(query_quad.shape, jnp.float32), (key_per_...]
    psum x6 -> x1, waiting for transfers between devices: 288 us -> 64.9 us  [per_device(): lax.psum(jnp.stack(part).astype(low), 'ctx').astype(full)]
    all_gather x4 -> x1, waiting for transfers between devices: 205 us -> 0.01 us  [per_device(): lax.all_gather(qkv_weight[layer], 'wa', axis=0, tiled=True)]
    dot_general x66 -> x10, matrix products: 177 us -> 17.1 us  [the longest x2 4.57 us: per_device(): jnp.dot(normed_two, gate_up_weight[layer, 1], preferred_element_type=full)]
    unnamed x18 -> x2, waiting for transfers between devices: 108 us -> 0.03 us
    reshape x17 -> x6, local copies, waits for them, and re-layouts: 56 us -> 4.96 us  [the longest x2 2.68 us: heads_out(): split = columns.reshape(KEY_VALUE_HEADS, HEAD_SIZE, -1, count)]
  transfers between devices with their start and end apart: 18 -> 2, of which waited for: 18 -> 1; matrix products, arithmetic and copies ran while one was open for 4% -> 4% of each run, Pallas kernels for 0% -> 20%
where the time goes in v1:
time: 780 us; the launch traced here: 778 us
  Pallas kernels  527 us (68%)
  waiting for transfers between devices  64.9 us (8%)
  other arithmetic  55.3 us (7%)
  matrix products  45 us (6%)
  local copies, waits for them, and re-layouts  42.9 us (6%)
  blocking collectives  27.2 us (3%)
  between operations  15.3 us (2%)
    pallas_call x24, Pallas kernels, run(): pl.pallas_call(functools.partial(exchange_kernel, kind, gather), out_shap...  451 us
    pallas_call x4, Pallas kernels, local_call(): pl.pallas_call(kernel, out_shape=[jax.ShapeDtypeStruct(s, t) for s, t in...  76 us
    psum x1, waiting for transfers between devices, per_device(): lax.psum(jnp.stack(part).astype(low), 'ctx').astype(full)  64.9 us
    all_gather x2, blocking collectives, per_device(): lax.all_gather(out_weight[layer], 'wa', axis=0, tiled=True)  27.2 us
    reduce_sum x11, other arithmetic, reduce(): jnp.sum(self.run(kind, False, x.astype(jnp.bfloat16)).astype(jnp.float32)...  24.2 us
  transfers between devices with their start and end apart: 2, of which 1 were waited for; matrix products, arithmetic and copies ran while one was open for 4% of the time, Pallas kernels for 20%

profile of v1, /device:TPU:0, one launch (start us, length us, event | category | flops | bytes accessed | tf_op | source)
XLA Modules:
  0.0 777.8 jit_solution(12275343119899777738)
XLA Ops:
  12.9 21.1 %shard_map.152 = bf16[4,144,960]{2,1,0:T(8,128)(2,1)} custom-call(bf16[144,960]{1,0:T(8,128)(2,1)} %get-tuple-element.93.x_ref), custom_call_target="tpu_custom_call" | custom-call | tf_op jit(solution)/shard_map/pallas_call | solution.py:115
  37.2 14.6 %all-gather = bf16[1,576,576]{2,1,0:T(8,128)(2,1)} all-gather(bf16[1,144,576]{2,1,0:T(8,128)(2,1)S(1)} %get-tuple-element.95), channel_id=2, replica_groups=mesh['ctx'=8,'wa'=4] {'wa'}, dimensions={1}, use_global_device_ids=true | all-gather | bytes 829440 | tf_op jit(solution)/shard_map/all_gather | solution.py:293
  53.3 10.4 %shard_map.153 = bf16[4,128,384]{2,1,0:T(8,128)(2,1)} custom-call(bf16[128,384]{1,0:T(8,128)(2,1)} %pad_maximum_fusion.13.x_ref), custom_call_target="tpu_custom_call" | custom-call | tf_op jit(solution)/shard_map/pallas_call | solution.py:115
  63.7 19.4 %shard_map.154 = bf16[4,512,384]{2,1,0:T(8,128)(2,1)} custom-call(bf16[512,384]{1,0:T(8,128)(2,1)} %bitcast.260), custom_call_target="tpu_custom_call" | custom-call | tf_op jit(solution)/shard_map/pallas_call | solution.py:115
  83.1 48.8 %shard_map.155 = bf16[2,2048,384]{2,1,0:T(8,128)(2,1)} custom-call(bf16[2048,384]{1,0:T(8,128)(2,1)} %bitcast.230), custom_call_target="tpu_custom_call" | custom-call | tf_op jit(solution)/shard_map/pallas_call | solution.py:115
  132.5 16.8 %shard_map.156 = (f32[3,64,384]{2,1,0:T(8,128)S(1)}, f32[3,1,384]{2,1,0:T(1,128)S(1)}) custom-call(bf16[3,384,64]{2,1,0:T(8,128)(2,1)S(1)} %bitcast.214, bf16[4096,384]{1,0:T(8,128)(2,1)} %bitcast.224, s32[4096,1]{1,0:T(8,128)S(1)} %copy.169.kpos_ref, s32[1,384]{1,0:T(1,128)S(1)} %bitcast.220), custom_call_target="tpu_custom_call" | custom-call | tf_op jit(solution)/shard_map/pallas_call | solution.py:221
  156.8 10.9 %shard_map.157 = bf16[4,128,576]{2,1,0:T(8,128)(2,1)} custom-call(bf16[128,576]{1,0:T(8,128)(2,1)} %multiply_convert_fusion.8.x_ref), custom_call_target="tpu_custom_call" | custom-call | tf_op jit(solution)/shard_map/pallas_call | solution.py:115
  176.6 9.2 %shard_map.158 = bf16[4,128,576]{2,1,0:T(8,128)(2,1)} custom-call(bf16[4,128,576]{2,1,0:T(8,128)(2,1)} %copy.172.x_ref), custom_call_target="tpu_custom_call" | custom-call | tf_op jit(solution)/shard_map/pallas_call | solution.py:115
  185.8 12.6 %all-gather.2 = bf16[1,576,576]{2,1,0:T(8,128)(2,1)} all-gather(bf16[1,144,576]{2,1,0:T(8,128)(2,1)S(1)} %copy-done.42), channel_id=4, replica_groups=mesh['ctx'=8,'wa'=4] {'wa'}, dimensions={1}, use_global_device_ids=true | all-gather | bytes 829440 | tf_op jit(solution)/shard_map/all_gather | solution.py:293
  212.0 9.3 %shard_map.159 = bf16[4,128,384]{2,1,0:T(8,128)(2,1)} custom-call(bf16[128,384]{1,0:T(8,128)(2,1)} %pad_maximum_fusion.14.x_ref), custom_call_target="tpu_custom_call" | custom-call | tf_op jit(solution)/shard_map/pallas_call | solution.py:115
  221.3 15.6 %shard_map.160 = bf16[4,512,384]{2,1,0:T(8,128)(2,1)} custom-call(bf16[512,384]{1,0:T(8,128)(2,1)} %bitcast.261), custom_call_target="tpu_custom_call" | custom-call | tf_op jit(solution)/shard_map/pallas_call | solution.py:115
  236.9 48.8 %shard_map.161 = bf16[2,2048,384]{2,1,0:T(8,128)(2,1)} custom-call(bf16[2048,384]{1,0:T(8,128)(2,1)} %bitcast.231), custom_call_target="tpu_custom_call" | custom-call | tf_op jit(solution)/shard_map/pallas_call | solution.py:115
  285.7 16.8 %shard_map.162 = (f32[3,64,384]{2,1,0:T(8,128)S(1)}, f32[3,1,384]{2,1,0:T(1,128)S(1)}) custom-call(bf16[3,384,64]{2,1,0:T(8,128)(2,1)S(1)} %bitcast.216, bf16[4096,384]{1,0:T(8,128)(2,1)} %bitcast.226, s32[4096,1]{1,0:T(8,128)S(1)} %copy.169.kpos_ref, s32[1,384]{1,0:T(1,128)S(1)} %bitcast.221), custom_call_target="tpu_custom_call" | custom-call | tf_op jit(solution)/shard_map/pallas_call | solution.py:221
  357.8 21.2 %shard_map.167 = (f32[3,64,384]{2,1,0:T(8,128)S(1)}, bf16[4096,384]{1,0:T(8,128)(2,1)}) custom-call(bf16[3,384,64]{2,1,0:T(8,128)(2,1)S(1)} %bitcast.217, bf16[3,384,64]{2,1,0:T(8,128)(2,1)S(1)} %bitcast.219, bf16[4096,384]{1,0:T(8,128)(2,1)} %bitcast.227, s32[4096,1]{1,0:T(8,128)S(1)} %copy.169.kpos_ref, s32[1,384]{1,0:T(1,128)S(1)} %bitcast.222, ...), custom_call_target="tpu_custom_call" | custom-call | tf_op jit(solution)/shard_map/pallas_call | solution.py:221
  379.0 48.8 %shard_map.168 = bf16[2,2048,384]{2,1,0:T(8,128)(2,1)} custom-call(bf16[2,2048,384]{2,1,0:T(8,128)(2,1)} %bitcast.241), custom_call_target="tpu_custom_call" | custom-call | tf_op jit(solution)/shard_map/pallas_call | solution.py:115
  431.9 16.2 %shard_map.169 = bf16[4,512,384]{2,1,0:T(8,128)(2,1)} custom-call(bf16[4,512,384]{2,1,0:T(8,128)(2,1)} %bitcast.228), custom_call_target="tpu_custom_call" | custom-call | tf_op jit(solution)/shard_map/pallas_call | solution.py:115
  450.6 12.5 %shard_map.170 = bf16[4,128,384]{2,1,0:T(8,128)(2,1)} custom-call(bf16[4,128,384]{2,1,0:T(8,128)(2,1)} %bitcast.252), custom_call_target="tpu_custom_call" | custom-call | tf_op jit(solution)/shard_map/pallas_call | solution.py:115
  505.2 21.2 %shard_map.173 = (f32[3,64,384]{2,1,0:T(8,128)S(1)}, bf16[4096,384]{1,0:T(8,128)(2,1)}) custom-call(bf16[3,384,64]{2,1,0:T(8,128)(2,1)S(1)} %bitcast.215, bf16[3,384,64]{2,1,0:T(8,128)(2,1)S(1)} %bitcast.218, bf16[4096,384]{1,0:T(8,128)(2,1)} %bitcast.225, s32[4096,1]{1,0:T(8,128)S(1)} %copy.169.kpos_ref, s32[1,384]{1,0:T(1,128)S(1)} %bitcast.223, ...), custom_call_target="tpu_custom_call" | custom-call | tf_op jit(solution)/shard_map/pallas_call | solution.py:221
  526.4 48.8 %shard_map.174 = bf16[2,2048,384]{2,1,0:T(8,128)(2,1)} custom-call(bf16[2,2048,384]{2,1,0:T(8,128)(2,1)} %bitcast.240), custom_call_target="tpu_custom_call" | custom-call | tf_op jit(solution)/shard_map/pallas_call | solution.py:115
  579.2 14.5 %shard_map.175 = bf16[4,512,384]{2,1,0:T(8,128)(2,1)} custom-call(bf16[4,512,384]{2,1,0:T(8,128)(2,1)} %bitcast.229), custom_call_target="tpu_custom_call" | custom-call | tf_op jit(solution)/shard_map/pallas_call | solution.py:115
  596.2 14.7 %shard_map.176 = bf16[4,128,384]{2,1,0:T(8,128)(2,1)} custom-call(bf16[4,128,384]{2,1,0:T(8,128)(2,1)} %bitcast.253), custom_call_target="tpu_custom_call" | custom-call | tf_op jit(solution)/shard_map/pallas_call | solution.py:115
  619.5 20.0 %shard_map.179 = bf16[4,160,1536]{2,1,0:T(8,128)(2,1)} custom-call(bf16[4,160,1536]{2,1,0:T(8,128)(2,1)} %fusion.x_ref), custom_call_target="tpu_custom_call" | custom-call | tf_op jit(solution)/shard_map/pallas_call | solution.py:115
  644.5 23.1 %shard_map.178 = bf16[4,160,1536]{2,1,0:T(8,128)(2,1)} custom-call(bf16[4,160,1536]{2,1,0:T(8,128)(2,1)} %fusion.1.x_ref), custom_call_target="tpu_custom_call" | custom-call | tf_op jit(solution)/shard_map/pallas_call | solution.py:115
  697.3 64.9 %all-reduce.3.cloned.1.call-done = (bf16[2,160,1536]{2,1,0:T(8,128)(2,1)}, bf16[2,2,576,384]{3,2,1,0:T(8,128)(2,1)}, bf16[2,384,576]{1,2,0:T(8,128)(2,1)}) async-done(((bf16[2,160,1536]{2,1,0:T(8,128)(2,1)}, bf16[2,2,576,384]{3,2,1,0:T(8,128)(2,1)}, bf16[2,384,576]{1,2,0:T(8,128)(2,1)}), (bf16[2,160,1536]{2,1,0:T(8,128)(2,1)}, bf16[2,2,576,384]{3,2,1,0:T(8,128)(2,1)}, ...) | async-done | bytes 3637264 | tf_op jit(solution)/shard_map/psum | solution.py:416
  (304 shorter events, 202.4 us)
Async XLA Ops:
  7.2 147.3 %copy-start = (bf16[512,576]{0,1:T(8,128)(2,1)S(1)}, bf16[512,576]{0,1:T(8,128)(2,1)}, u32[]{:S(2)}) copy-start(bf16[512,576]{0,1:T(8,128)(2,1)} %param.17) | copy-start | bytes 1769476
  7.2 193.2 %all-gather.5.cloned.1.call-start = ((), (), s32[]{:S(2)}) async-start(), calls=%async_computation | async-start | bytes 1474560 | tf_op jit(solution)/shard_map/all_gather | solution.py:291
  9.2 752.9 %all-reduce.3.cloned.1.call-start = ((), (), s32[]{:S(2)}) async-start(), calls=%async_computation.1 | async-start | bytes 7274496 | tf_op jit(solution)/shard_map/psum | solution.py:416
  11.6 188.8 %copy-start.53 = (f32[576]{0:T(1024)}, f32[576]{0:T(1024)S(1)}, u32[]{:S(2)}) copy-start(f32[576]{0:T(1024)S(1)} %get-tuple-element.74) | copy-start | bytes 6916
  12.9 23.2 %copy-start.61 = (f32[128]{0:T(128)}, f32[128]{0:T(128)S(1)}, u32[]{:S(2)}) copy-start(f32[128]{0:T(128)S(1)} %add_rsqrt_fusion.3) | copy-start | bytes 1540
  12.9 23.3 %copy-start.55 = (bf16[2,576]{1,0:T(2,128)(2,1)S(1)}, bf16[2,576]{1,0:T(2,128)(2,1)}, u32[]{:S(2)}) copy-start(bf16[2,576]{1,0:T(2,128)(2,1)} %param.14) | copy-start | bytes 6916
  36.3 116.7 %copy-start.51 = (f32[576]{0:T(1024)}, f32[576]{0:T(1024)S(1)}, u32[]{:S(2)}) copy-start(f32[576]{0:T(1024)S(1)} %get-tuple-element.73) | copy-start | bytes 6916
  151.2 16.5 %copy-start.22 = (f32[128,3,3,64]{0,3,2,1:T(8,128)}, f32[128,3,3,64]{0,3,2,1:T(8,128)S(1)}, u32[]{:S(2)}) copy-start(f32[128,3,3,64]{0,3,2,1:T(8,128)S(1)} %copy.170) | copy-start | bytes 884740
  153.0 16.6 %copy-start.59 = (f32[128]{0:T(128)}, f32[128]{0:T(128)S(1)}, u32[]{:S(2)}) copy-start(f32[128]{0:T(128)S(1)} %add_rsqrt_fusion.2) | copy-start | bytes 1540
  173.1 12.7 %copy-start.42 = (bf16[1,144,576]{2,1,0:T(8,128)(2,1)S(1)}, bf16[1,144,576]{2,1,0:T(8,128)(2,1)}, u32[]{:S(2)}) copy-start(bf16[1,144,576]{2,1,0:T(8,128)(2,1)} %get-tuple-element.94) | copy-start | bytes 497668
  185.8 13.8 %copy-start.5 = (f32[128,576]{1,0:T(8,128)S(1)}, f32[128,576]{1,0:T(8,128)}, u32[]{:S(2)}) copy-start(f32[128,576]{1,0:T(8,128)} %copy-done.4) | copy-start | bytes 884740
  200.4 6.5 copy-start.57
  323.6 3.9 copy-start.48
  343.5 9.6 %copy-start.17 = (f32[128,576]{1,0:T(8,128)S(1)}, f32[128,576]{1,0:T(8,128)}, u32[]{:S(2)}) copy-start(f32[128,576]{1,0:T(8,128)} %copy-done.16) | copy-start | bytes 884740
  343.5 10.3 %copy-start.43 = (bf16[128,576]{1,0:T(8,128)(2,1)S(1)}, bf16[128,576]{1,0:T(8,128)(2,1)}, u32[]{:S(2)}) copy-start(bf16[128,576]{1,0:T(8,128)(2,1)} %copy.212) | copy-start | bytes 442372
  464.2 3.9 copy-start.54
  464.2 3.9 copy-start.58
  466.0 4.7 copy-start.3
  466.0 4.7 copy-start.37
  483.3 3.8 copy-start.10
  490.2 11.4 %copy-start.6 = (f32[128,576]{1,0:T(8,128)S(1)}, f32[128,576]{1,0:T(8,128)}, u32[]{:S(2)}) copy-start(f32[128,576]{1,0:T(8,128)} %copy-done.4) | copy-start | bytes 884740
  490.2 11.4 %copy-start.52 = (f32[576]{0:T(1024)S(1)}, f32[576]{0:T(1024)}, u32[]{:S(2)}) copy-start(f32[576]{0:T(1024)} %copy-done.51) | copy-start | bytes 6916
  490.2 11.4 %copy-start.60 = (f32[128]{0:T(128)S(1)}, f32[128]{0:T(128)}, u32[]{:S(2)}) copy-start(f32[128]{0:T(128)} %copy-done.59) | copy-start | bytes 1540
  763.1 4.5 copy-start.31
  (42 other events, 87.7 us)
Sparse Core Ops, SparseCore 0:
  10.4 36.8 all-gather.4
  673.6 88.5 all-reduce.2

commit v2 on v1

--- a/solution.py
+++ b/solution.py
@@ -17,6 +17,7 @@
 EPSILON = 1e-05
 KEY_CHUNK = 512
 VMEM_BYTES = 50 * 1024 * 1024
+LINK_VMEM_BYTES = 24 * 1024 * 1024
 
 
 def rotation(token_pos, head_width):
@@ -66,6 +67,8 @@
     ctx_at = lax.axis_index("ctx")
     if kind == "wa":
         return lax.axis_size("wa"), lax.axis_index("wa"), lambda p: {"wa": p}
+    if kind == "ctx":
+        return lax.axis_size("ctx"), ctx_at, lambda p: {"ctx": p}
     core = lax.rem(ctx_at, 2)
     if kind == "core":
         return 2, core, lambda p: {"ctx": ctx_at - core + p}
@@ -115,15 +118,17 @@
         return pl.pallas_call(
             functools.partial(exchange_kernel, kind, gather),
             out_shape=jax.ShapeDtypeStruct(out_shape, x.dtype),
-            in_specs=[pl.BlockSpec(memory_space=pl.ANY)],
-            out_specs=pl.BlockSpec(memory_space=pl.ANY),
+            in_specs=[pl.BlockSpec(memory_space=pltpu.VMEM)],
+            out_specs=pl.BlockSpec(memory_space=pltpu.VMEM),
             scratch_shapes=[
                 pltpu.SemaphoreType.DMA,
                 pltpu.SemaphoreType.DMA((count - 1,)),
                 pltpu.SemaphoreType.DMA((count - 1,)),
             ],
             compiler_params=pltpu.CompilerParams(
-                collective_id=collective, has_side_effects=True
+                collective_id=collective,
+                has_side_effects=True,
+                vmem_limit_bytes=LINK_VMEM_BYTES,
             ),
         )(x)
 
@@ -132,6 +137,18 @@
 
     def reduce(self, kind, x):
         return jnp.sum(self.run(kind, False, x.astype(jnp.bfloat16)).astype(jnp.float32), axis=0)
+
+
+def sum_over_ctx(links, x):
+    count = lax.axis_size("ctx")
+    high, wide = x.shape
+    tiles = x.reshape(high // 16, 16, wide // 128, 128).transpose(0, 2, 1, 3).reshape(-1, 16, 128)
+    number = tiles.shape[0]
+    tiles = jnp.pad(tiles.astype(jnp.bfloat16), ((0, -number % count), (0, 0), (0, 0)))
+    part = links.reduce("ctx", tiles.reshape(count, -1, 128))
+    total = links.gather("ctx", part.astype(jnp.bfloat16)).reshape(-1, 16, 128)[:number]
+    total = total.reshape(high // 16, wide // 128, 16, 128).transpose(0, 2, 1, 3)
+    return total.reshape(high, wide)
 
 
 def dot_of(left, right, left_dim, right_dim):
@@ -286,11 +303,12 @@
             own_rows, heads * HEAD_SIZE
         )
 
-    qkv_full = [links.gather("wa", qkv_weight[0]).reshape(width, -1)]
-    qkv_full += [
-        lax.all_gather(qkv_weight[layer], "wa", axis=0, tiled=True) for layer in range(1, LAYERS)
-    ]
-    out_full = [lax.all_gather(out_weight[layer], "wa", axis=0, tiled=True) for layer in range(LAYERS)]
+    qkv_cols = qkv_weight.shape[2]
+    slab = qkv_weight.shape[1]
+    later = jnp.concatenate([out_weight[0], out_weight[1], qkv_weight[1]], axis=1)
+    later = lax.all_gather(later, "wa", axis=0, tiled=True)
+    out_full = [later[:, :width], later[:, width : 2 * width]]
+    qkv_full = [links.gather("wa", qkv_weight[0]).reshape(width, -1), later[:, 2 * width :]]
     residual = own(hidden_in).astype(full)
     stored = []
     for layer in range(LAYERS):
@@ -338,7 +356,7 @@
             + (middle, inv_two, gain_two, normed_two, gate, up, activated)
         )
         residual = output_rows
-    hidden_out = gather_rows(residual).astype(full)
+    hidden_own = residual.astype(low)
     gradient = own(out_grad).astype(full)
     grad_low = out_grad
     row_grads = [None] * LAYERS
@@ -361,6 +379,9 @@
             contract_cols(dgate, gate_up_weight[layer, 0])
             + contract_cols(dup, gate_up_weight[layer, 1])
         )
+        if layer == 0:
+            early = (row_grads[1].astype(low), jnp.stack(gate_up_grads).astype(low))
+            early = lax.psum(early + (jnp.stack(down_grads).astype(low),), "ctx")
         gain_two_grad, dmiddle = norm_backward(dnormed_two, middle, inv_two, gain_two)
         grad_mid = gradient + dmiddle
         mid_low = grad_mid.astype(low)
@@ -410,13 +431,13 @@
         pad_rows = 16 + (-block.shape[1]) % 16
         gains = jnp.broadcast_to(gains, (wa_count, pad_rows, gains.shape[0]))
         row_grads[layer] = links.reduce("wa", jnp.concatenate([block, gains], axis=1))
-    input_grad = gather_rows(gradient).astype(full)
-    slab = qkv_weight.shape[1]
-    rows_sum, gate_up_sum, down_sum = (
-        lax.psum(jnp.stack(part).astype(low), "ctx").astype(full)
-        for part in (row_grads, gate_up_grads, down_grads)
-    )
-    qkv_cols = qkv_weight.shape[2]
+        if layer > 0:
+            grad_low, row_grads[layer] = lax.optimization_barrier((grad_low, row_grads[layer]))
+    ends = links.gather("wa", jnp.stack([hidden_own, gradient.astype(low)])).astype(full)
+    hidden_out, input_grad = (ends[:, at].reshape(row_count, width) for at in range(2))
+    rows_sum = jnp.stack([sum_over_ctx(links, row_grads[0]), early[0]]).astype(full)
+    gate_up_sum = early[1].astype(full)
+    down_sum = early[2].astype(full)
     return (
         hidden_out,
         input_grad,

time: 780 us -> 584 us (0.75)
  Pallas kernels: 527 us -> 412 us
  waiting for transfers between devices: 64.9 us -> 7.68 us
  blocking collectives: 27.2 us -> 0 us
  local copies, waits for them, and re-layouts: 42.9 us -> 64.8 us
  other arithmetic: 55.3 us -> 33.7 us
    pallas_call x24 -> x25, Pallas kernels: 451 us -> 337 us  [run(): pl.pallas_call(functools.partial(exchange_kernel, kind, gather), out_shap...]
    psum x1, waiting for transfers between devices: 64.9 us -> 7.64 us  [per_device(): early = lax.psum(early + (jnp.stack(down_grads).astype(low),), 'ctx')]
    all_gather x2 -> x0, blocking collectives: 27.2 us -> none  [per_device(): lax.all_gather(out_weight[layer], 'wa', axis=0, tiled=True)]
    unnamed x138 -> x174, local copies, waits for them, and re-layouts: 12.7 us -> 32.8 us
    reduce_sum x11 -> x13, other arithmetic: 24.2 us -> 11.9 us  [reduce(): jnp.sum(self.run(kind, False, x.astype(jnp.bfloat16)).astype(jnp.float32)...]
  transfers between devices with their start and end apart: 2 -> 2, of which waited for: 1 -> 1; matrix products, arithmetic and copies ran while one was open for 4% -> 3% of each run, Pallas kernels for 20% -> 27%
where the time goes in v2:
time: 584 us; the launch traced here: 575 us
  Pallas kernels  412 us (71%)
  local copies, waits for them, and re-layouts  64.8 us (11%)
  matrix products  40.3 us (7%)
  other arithmetic  33.7 us (6%)
  between operations  15.9 us (3%)
  waiting for transfers between devices  7.68 us (1%)
    pallas_call x25, Pallas kernels, run(): pl.pallas_call(functools.partial(exchange_kernel, kind, gather), out_shap...  337 us
    pallas_call x4, Pallas kernels, local_call(): pl.pallas_call(kernel, out_shape=[jax.ShapeDtypeStruct(s, t) for s, t in...  75.5 us
    unnamed x174, local copies, waits for them, and re-layouts  32.8 us
    dot_general x10, matrix products, contract_cols(): lax.dot_general(left, right, (((1,), (1,)), ((), ())), preferred_element_...  15.8 us
    dot_general x10, matrix products, contract_rows(): lax.dot_general(left, right, (((0,), (0,)), ((), ())), preferred_element_...  12.3 us
    reduce_sum x13, other arithmetic, reduce(): jnp.sum(self.run(kind, False, x.astype(jnp.bfloat16)).astype(jnp.float32)...  11.9 us
  transfers between devices with their start and end apart: 2, of which 1 were waited for; matrix products, arithmetic and copies ran while one was open for 3% of the time, Pallas kernels for 27%

profile of v2, /device:TPU:0, one launch (start us, length us, event | category | flops | bytes accessed | tf_op | source)
XLA Modules:
  0.0 574.6 jit_solution(1875740707739142798)
XLA Ops:
  12.0 24.4 %shard_map.152 = bf16[4,144,960]{2,1,0:T(8,128)(2,1)S(1)} custom-call(bf16[144,960]{1,0:T(8,128)(2,1)S(1)} %get-tuple-element.99.x_ref), custom_call_target="tpu_custom_call" | custom-call | tf_op jit(solution)/shard_map/pallas_call | solution.py:118
  40.2 10.2 %shard_map.153 = bf16[4,128,384]{2,1,0:T(8,128)(2,1)S(1)} custom-call(bf16[128,384]{1,0:T(8,128)(2,1)S(1)} %pad_maximum_fusion.13.x_ref), custom_call_target="tpu_custom_call" | custom-call | tf_op jit(solution)/shard_map/pallas_call | solution.py:118
  50.4 24.2 %shard_map.154 = bf16[4,512,384]{2,1,0:T(8,128)(2,1)S(1)} custom-call(bf16[512,384]{1,0:T(8,128)(2,1)S(1)} %bitcast.234), custom_call_target="tpu_custom_call" | custom-call | tf_op jit(solution)/shard_map/pallas_call | solution.py:118
  80.6 16.8 %shard_map.156 = (f32[3,64,384]{2,1,0:T(8,128)S(1)}, f32[3,1,384]{2,1,0:T(1,128)S(1)}) custom-call(bf16[3,384,64]{2,1,0:T(8,128)(2,1)S(1)} %bitcast.214, bf16[4096,384]{1,0:T(8,128)(2,1)} %bitcast.202, s32[4096,1]{1,0:T(8,128)S(1)} %copy.176.kpos_ref, s32[1,384]{1,0:T(1,128)S(1)} %bitcast.238), custom_call_target="tpu_custom_call" | custom-call | tf_op jit(solution)/shard_map/pallas_call | solution.py:238
  104.6 11.0 %shard_map.157 = bf16[4,128,576]{2,1,0:T(8,128)(2,1)S(1)} custom-call(bf16[128,576]{1,0:T(8,128)(2,1)S(1)} %multiply_convert_fusion.8.x_ref), custom_call_target="tpu_custom_call" | custom-call | tf_op jit(solution)/shard_map/pallas_call | solution.py:118
  123.0 10.0 %shard_map.158 = bf16[4,128,576]{2,1,0:T(8,128)(2,1)S(1)} custom-call(bf16[4,128,576]{2,1,0:T(8,128)(2,1)S(1)} %copy-done.12), custom_call_target="tpu_custom_call" | custom-call | tf_op jit(solution)/shard_map/pallas_call | solution.py:118
  142.7 10.4 %shard_map.159 = bf16[4,128,384]{2,1,0:T(8,128)(2,1)S(1)} custom-call(bf16[128,384]{1,0:T(8,128)(2,1)S(1)} %pad_maximum_fusion.14.x_ref), custom_call_target="tpu_custom_call" | custom-call | tf_op jit(solution)/shard_map/pallas_call | solution.py:118
  153.0 20.4 %shard_map.160 = bf16[4,512,384]{2,1,0:T(8,128)(2,1)S(1)} custom-call(bf16[512,384]{1,0:T(8,128)(2,1)S(1)} %bitcast.235), custom_call_target="tpu_custom_call" | custom-call | tf_op jit(solution)/shard_map/pallas_call | solution.py:118
  178.6 16.8 %shard_map.162 = (f32[3,64,384]{2,1,0:T(8,128)S(1)}, f32[3,1,384]{2,1,0:T(1,128)S(1)}) custom-call(bf16[3,384,64]{2,1,0:T(8,128)(2,1)S(1)} %bitcast.216, bf16[4096,384]{1,0:T(8,128)(2,1)} %bitcast.204, s32[4096,1]{1,0:T(8,128)S(1)} %copy.176.kpos_ref, s32[1,384]{1,0:T(1,128)S(1)} %bitcast.239), custom_call_target="tpu_custom_call" | custom-call | tf_op jit(solution)/shard_map/pallas_call | solution.py:238
  202.5 10.6 %shard_map.163 = bf16[4,128,576]{2,1,0:T(8,128)(2,1)S(1)} custom-call(bf16[128,576]{1,0:T(8,128)(2,1)S(1)} %multiply_convert_fusion.6.x_ref), custom_call_target="tpu_custom_call" | custom-call | tf_op jit(solution)/shard_map/pallas_call | solution.py:118
  224.3 10.2 %shard_map.164 = bf16[4,128,576]{2,1,0:T(8,128)(2,1)S(1)} custom-call(bf16[4,128,576]{2,1,0:T(8,128)(2,1)S(1)} %copy-done.13), custom_call_target="tpu_custom_call" | custom-call | tf_op jit(solution)/shard_map/pallas_call | solution.py:118
  240.9 9.9 %shard_map.165 = bf16[4,128,576]{2,1,0:T(8,128)(2,1)S(1)} custom-call(bf16[4,128,576]{2,1,0:T(8,128)(2,1)S(1)} %bitcast.228), custom_call_target="tpu_custom_call" | custom-call | tf_op jit(solution)/shard_map/pallas_call | solution.py:118
  259.2 21.0 %shard_map.166 = (f32[3,64,384]{2,1,0:T(8,128)S(1)}, bf16[4096,384]{1,0:T(8,128)(2,1)}) custom-call(bf16[3,384,64]{2,1,0:T(8,128)(2,1)S(1)} %bitcast.217, bf16[3,384,64]{2,1,0:T(8,128)(2,1)S(1)} %bitcast.237, bf16[4096,384]{1,0:T(8,128)(2,1)} %bitcast.205, s32[4096,1]{1,0:T(8,128)S(1)} %copy.176.kpos_ref, s32[1,384]{1,0:T(1,128)S(1)} %bitcast.240, ...), custom_call_target="tpu_custom_call" | custom-call | tf_op jit(solution)/shard_map/pallas_call | solution.py:238
  293.5 20.5 %shard_map.168 = bf16[4,512,384]{2,1,0:T(8,128)(2,1)S(1)} custom-call(bf16[4,512,384]{2,1,0:T(8,128)(2,1)S(1)} %bitcast.206), custom_call_target="tpu_custom_call" | custom-call | tf_op jit(solution)/shard_map/pallas_call | solution.py:118
  318.7 11.5 %shard_map.169 = bf16[4,128,384]{2,1,0:T(8,128)(2,1)S(1)} custom-call(bf16[4,128,384]{2,1,0:T(8,128)(2,1)S(1)} %bitcast.232), custom_call_target="tpu_custom_call" | custom-call | tf_op jit(solution)/shard_map/pallas_call | solution.py:118
  355.1 20.5 %shard_map.171 = bf16[4,160,1536]{2,1,0:T(8,128)(2,1)S(1)} custom-call(bf16[4,160,1536]{2,1,0:T(8,128)(2,1)S(1)} %fusion.1.x_ref), custom_call_target="tpu_custom_call" | custom-call | tf_op jit(solution)/shard_map/pallas_call | solution.py:118
  384.6 10.0 %shard_map.172 = bf16[4,128,576]{2,1,0:T(8,128)(2,1)S(1)} custom-call(bf16[4,128,576]{2,1,0:T(8,128)(2,1)S(1)} %bitcast.229), custom_call_target="tpu_custom_call" | custom-call | tf_op jit(solution)/shard_map/pallas_call | solution.py:118
  397.5 20.9 %shard_map.173 = (f32[3,64,384]{2,1,0:T(8,128)S(1)}, bf16[4096,384]{1,0:T(8,128)(2,1)}) custom-call(bf16[3,384,64]{2,1,0:T(8,128)(2,1)S(1)} %bitcast.215, bf16[3,384,64]{2,1,0:T(8,128)(2,1)S(1)} %bitcast.236, bf16[4096,384]{1,0:T(8,128)(2,1)} %bitcast.203, s32[4096,1]{1,0:T(8,128)S(1)} %copy.176.kpos_ref, s32[1,384]{1,0:T(1,128)S(1)} %bitcast.241, ...), custom_call_target="tpu_custom_call" | custom-call | tf_op jit(solution)/shard_map/pallas_call | solution.py:238
  427.4 20.4 %shard_map.175 = bf16[4,512,384]{2,1,0:T(8,128)(2,1)S(1)} custom-call(bf16[4,512,384]{2,1,0:T(8,128)(2,1)S(1)} %bitcast.207), custom_call_target="tpu_custom_call" | custom-call | tf_op jit(solution)/shard_map/pallas_call | solution.py:118
  448.2 15.0 %shard_map.176 = bf16[4,128,384]{2,1,0:T(8,128)(2,1)S(1)} custom-call(bf16[4,128,384]{2,1,0:T(8,128)(2,1)S(1)} %bitcast.233), custom_call_target="tpu_custom_call" | custom-call | tf_op jit(solution)/shard_map/pallas_call | solution.py:118
  470.9 21.2 %shard_map.178 = bf16[4,160,1536]{2,1,0:T(8,128)(2,1)S(1)} custom-call(bf16[4,160,1536]{2,1,0:T(8,128)(2,1)S(1)} %fusion.x_ref), custom_call_target="tpu_custom_call" | custom-call | tf_op jit(solution)/shard_map/pallas_call | solution.py:118
  492.9 16.9 %shard_map.179 = bf16[8,240,128]{2,1,0:T(8,128)(2,1)S(1)} custom-call(bf16[8,240,128]{2,1,0:T(8,128)(2,1)S(1)} %bitcast.230), custom_call_target="tpu_custom_call" | custom-call | tf_op jit(solution)/shard_map/pallas_call | solution.py:118
  509.8 19.2 %shard_map.180 = bf16[8,240,128]{2,1,0:T(8,128)(2,1)S(1)} custom-call(bf16[240,128]{1,0:T(8,128)(2,1)S(1)} %reduce_sum.287.x_ref), custom_call_target="tpu_custom_call" | custom-call | tf_op jit(solution)/shard_map/pallas_call | solution.py:118
  530.0 17.8 %shard_map.177 = bf16[4,2,128,576]{3,2,1,0:T(8,128)(2,1)S(1)} custom-call(bf16[2,128,576]{2,1,0:T(8,128)(2,1)S(1)} %pad_maximum_fusion.4.x_ref), custom_call_target="tpu_custom_call" | custom-call | tf_op jit(solution)/shard_map/pallas_call | solution.py:118
  (345 shorter events, 168.9 us)
Async XLA Ops:
  7.2 94.9 %all-gather.2.cloned.1.call-start = ((), (), s32[]{:S(2)}) async-start(), calls=%async_computation | async-start | bytes 3133440 | tf_op jit(solution)/shard_map/all_gather | solution.py:309
  10.4 26.0 %copy-start.70 = (bf16[2,576]{1,0:T(2,128)(2,1)S(1)}, bf16[2,576]{1,0:T(2,128)(2,1)}, u32[]{:S(2)}) copy-start(bf16[2,576]{1,0:T(2,128)(2,1)} %param.11) | copy-start | bytes 6916
  10.5 548.0 %all-reduce.3.cloned.1.call-start = ((), (), s32[]{:S(2)}) async-start(), calls=%async_computation.1 | async-start | bytes 6291456 | tf_op jit(solution)/shard_map/psum | solution.py:384
  12.0 90.1 %copy-start.23 = (bf16[128,576]{1,0:T(8,128)(2,1)}, bf16[128,576]{1,0:T(8,128)(2,1)S(1)}, u32[]{:S(2)}) copy-start(bf16[128,576]{1,0:T(8,128)(2,1)S(1)} %copy.220) | copy-start | bytes 442372
  36.5 97.4 %copy-start.68 = (f32[576]{0:T(1024)}, f32[576]{0:T(1024)S(1)}, u32[]{:S(2)}) copy-start(f32[576]{0:T(1024)S(1)} %get-tuple-element.78) | copy-start | bytes 6916
  80.5 18.7 %copy-start.71 = (bf16[2,576]{1,0:T(2,128)(2,1)S(1)}, bf16[2,576]{1,0:T(2,128)(2,1)}, u32[]{:S(2)}) copy-start(bf16[2,576]{1,0:T(2,128)(2,1)} %param.14) | copy-start | bytes 6916
  99.3 4.5 copy-start.35
  99.3 4.5 copy-start.66
  102.1 13.6 %copy-start.32 = (bf16[2,2,576,384]{3,2,1,0:T(8,128)(2,1)S(1)}, bf16[2,2,576,384]{3,2,1,0:T(8,128)(2,1)}, u32[]{:S(2)}) copy-start(bf16[2,2,576,384]{3,2,1,0:T(8,128)(2,1)} %param.15) | copy-start | bytes 5308420
  103.8 13.8 %copy-start.75 = (f32[128]{0:T(128)}, f32[128]{0:T(128)S(1)}, u32[]{:S(2)}) copy-start(f32[128]{0:T(128)S(1)} %add_rsqrt_fusion.2) | copy-start | bytes 1540
  122.9 10.1 %copy-start.21 = (f32[128,576]{1,0:T(8,128)S(1)}, f32[128,576]{1,0:T(8,128)}, u32[]{:S(2)}) copy-start(f32[128,576]{1,0:T(8,128)} %copy-done.20) | copy-start | bytes 884740
  199.7 13.4 %copy-start.33 = (bf16[2,2,576,384]{3,2,1,0:T(8,128)(2,1)S(1)}, bf16[2,2,576,384]{3,2,1,0:T(8,128)(2,1)}, u32[]{:S(2)}) copy-start(bf16[2,2,576,384]{3,2,1,0:T(8,128)(2,1)} %param.15) | copy-start | bytes 5308420
  201.7 11.9 %copy-start.80 = (f32[512,384]{1,0:T(8,128)S(1)}, f32[512,384]{1,0:T(8,128)}, u32[]{:S(2)}) copy-start(f32[512,384]{1,0:T(8,128)} %fusion.19) | copy-start | bytes 2359300
  224.3 11.0 %copy-start.31 = (f32[512,576]{0,1:T(8,128)S(1)}, f32[512,576]{0,1:T(8,128)}, u32[]{:S(2)}) copy-start(f32[512,576]{0,1:T(8,128)} %fusion.24) | copy-start | bytes 3538948
  224.3 11.0 %copy-start.64 = (bf16[512,384]{1,0:T(8,128)(2,1)S(1)}, bf16[512,384]{1,0:T(8,128)(2,1)}, u32[]{:S(2)}) copy-start(bf16[512,384]{1,0:T(8,128)(2,1)} %copy-done.63) | copy-start | bytes 1179652
  240.9 10.0 %copy-start.30 = (f32[128,576]{1,0:T(8,128)S(1)}, f32[128,576]{1,0:T(8,128)}, u32[]{:S(2)}) copy-start(f32[128,576]{1,0:T(8,128)} %copy-done.29) | copy-start | bytes 884740
  240.9 10.0 %copy-start.49 = (f32[128,576]{1,0:T(8,128)S(1)}, f32[128,576]{1,0:T(8,128)}, u32[]{:S(2)}) copy-start(f32[128,576]{1,0:T(8,128)} %convert_reduce_fusion.3) | copy-start | bytes 884740
  240.9 11.3 %copy-start.58 = (bf16[128,576]{1,0:T(8,128)(2,1)S(1)}, bf16[128,576]{1,0:T(8,128)(2,1)}, u32[]{:S(2)}) copy-start(bf16[128,576]{1,0:T(8,128)(2,1)} %copy.221) | copy-start | bytes 442372
  315.1 15.9 %copy-start.18 = (f32[3,64,384]{2,1,0:T(8,128)S(1)}, f32[3,64,384]{2,1,0:T(8,128)}, u32[]{:S(2)}) copy-start(f32[3,64,384]{2,1,0:T(8,128)} %copy-done.17) | copy-start | bytes 884740
  341.1 11.9 %copy-start.72 = (bf16[576]{0:T(1024)(128)(2,1)S(1)}, bf16[576]{0:T(1024)(128)(2,1)}, u32[]{:S(2)}) copy-start(bf16[576]{0:T(1024)(128)(2,1)} %get-tuple-element.70) | copy-start | bytes 3460
  383.2 11.6 %copy-start.22 = (f32[128,576]{1,0:T(8,128)S(1)}, f32[128,576]{1,0:T(8,128)}, u32[]{:S(2)}) copy-start(f32[128,576]{1,0:T(8,128)} %copy-done.20) | copy-start | bytes 884740
  383.2 11.6 %copy-start.67 = (f32[576]{0:T(1024)S(1)}, f32[576]{0:T(1024)}, u32[]{:S(2)}) copy-start(f32[576]{0:T(1024)} %copy-done.66) | copy-start | bytes 6916
  383.2 11.6 %copy-start.76 = (f32[128]{0:T(128)S(1)}, f32[128]{0:T(128)}, u32[]{:S(2)}) copy-start(f32[128]{0:T(128)} %copy-done.75) | copy-start | bytes 1540
  384.6 10.4 %copy-start.48 = (f32[128,576]{1,0:T(8,128)S(1)}, f32[128,576]{1,0:T(8,128)}, u32[]{:S(2)}) copy-start(f32[128,576]{1,0:T(8,128)} %get-tuple-element.84) | copy-start | bytes 884740
  (60 other events, 106.5 us)
Sparse Core Ops, SparseCore 0:
  10.6 59.9 all-gather.1
  467.7 90.7 all-reduce.2

commit v3 on v2

--- a/solution.py
+++ b/solution.py
@@ -15,7 +15,7 @@
 
 
 EPSILON = 1e-05
-KEY_CHUNK = 512
+KEY_CHUNK = 1024
 VMEM_BYTES = 50 * 1024 * 1024
 LINK_VMEM_BYTES = 24 * 1024 * 1024
 

time: 584 us -> 571 us (0.978)
  Pallas kernels: 412 us -> 398 us
    pallas_call x4, Pallas kernels: 75.5 us -> 61.7 us  [local_call(): pl.pallas_call(kernel, out_shape=[jax.ShapeDtypeStruct(s, t) for s, t in...]
where the time goes in v3:
time: 571 us; the launch traced here: 561 us
  Pallas kernels  398 us (70%)
  local copies, waits for them, and re-layouts  64.8 us (11%)
  matrix products  40.4 us (7%)
  other arithmetic  33.7 us (6%)
  between operations  15.9 us (3%)
  waiting for transfers between devices  7.68 us (1%)
    pallas_call x25, Pallas kernels, run(): pl.pallas_call(functools.partial(exchange_kernel, kind, gather), out_shap...  336 us
    pallas_call x4, Pallas kernels, local_call(): pl.pallas_call(kernel, out_shape=[jax.ShapeDtypeStruct(s, t) for s, t in...  61.7 us
    unnamed x174, local copies, waits for them, and re-layouts  32.8 us
    dot_general x10, matrix products, contract_cols(): lax.dot_general(left, right, (((1,), (1,)), ((), ())), preferred_element_...  15.8 us
    dot_general x10, matrix products, contract_rows(): lax.dot_general(left, right, (((0,), (0,)), ((), ())), preferred_element_...  12.3 us
    reduce_sum x13, other arithmetic, reduce(): jnp.sum(self.run(kind, False, x.astype(jnp.bfloat16)).astype(jnp.float32)...  11.9 us
  transfers between devices with their start and end apart: 2, of which 1 were waited for; matrix products, arithmetic and copies ran while one was open for 3% of the time, Pallas kernels for 27%

profile of v3, /device:TPU:0, one launch (start us, length us, event | category | flops | bytes accessed | tf_op | source)
XLA Modules:
  0.0 560.6 jit_solution(6967208121104738112)
XLA Ops:
  12.0 24.4 %shard_map.152 = bf16[4,144,960]{2,1,0:T(8,128)(2,1)S(1)} custom-call(bf16[144,960]{1,0:T(8,128)(2,1)S(1)} %get-tuple-element.99.x_ref), custom_call_target="tpu_custom_call" | custom-call | tf_op jit(solution)/shard_map/pallas_call | solution.py:118
  40.2 10.2 %shard_map.153 = bf16[4,128,384]{2,1,0:T(8,128)(2,1)S(1)} custom-call(bf16[128,384]{1,0:T(8,128)(2,1)S(1)} %pad_maximum_fusion.13.x_ref), custom_call_target="tpu_custom_call" | custom-call | tf_op jit(solution)/shard_map/pallas_call | solution.py:118
  50.4 24.2 %shard_map.154 = bf16[4,512,384]{2,1,0:T(8,128)(2,1)S(1)} custom-call(bf16[512,384]{1,0:T(8,128)(2,1)S(1)} %bitcast.234), custom_call_target="tpu_custom_call" | custom-call | tf_op jit(solution)/shard_map/pallas_call | solution.py:118
  80.6 13.0 %shard_map.156 = (f32[3,64,384]{2,1,0:T(8,128)S(1)}, f32[3,1,384]{2,1,0:T(1,128)S(1)}) custom-call(bf16[3,384,64]{2,1,0:T(8,128)(2,1)S(1)} %bitcast.214, bf16[4096,384]{1,0:T(8,128)(2,1)} %bitcast.202, s32[4096,1]{1,0:T(8,128)S(1)} %copy.176.kpos_ref, s32[1,384]{1,0:T(1,128)S(1)} %bitcast.238), custom_call_target="tpu_custom_call" | custom-call | tf_op jit(solution)/shard_map/pallas_call | solution.py:238
  100.8 11.0 %shard_map.157 = bf16[4,128,576]{2,1,0:T(8,128)(2,1)S(1)} custom-call(bf16[128,576]{1,0:T(8,128)(2,1)S(1)} %multiply_convert_fusion.8.x_ref), custom_call_target="tpu_custom_call" | custom-call | tf_op jit(solution)/shard_map/pallas_call | solution.py:118
  119.1 10.0 %shard_map.158 = bf16[4,128,576]{2,1,0:T(8,128)(2,1)S(1)} custom-call(bf16[4,128,576]{2,1,0:T(8,128)(2,1)S(1)} %copy-done.12), custom_call_target="tpu_custom_call" | custom-call | tf_op jit(solution)/shard_map/pallas_call | solution.py:118
  138.8 10.4 %shard_map.159 = bf16[4,128,384]{2,1,0:T(8,128)(2,1)S(1)} custom-call(bf16[128,384]{1,0:T(8,128)(2,1)S(1)} %pad_maximum_fusion.14.x_ref), custom_call_target="tpu_custom_call" | custom-call | tf_op jit(solution)/shard_map/pallas_call | solution.py:118
  149.2 20.3 %shard_map.160 = bf16[4,512,384]{2,1,0:T(8,128)(2,1)S(1)} custom-call(bf16[512,384]{1,0:T(8,128)(2,1)S(1)} %bitcast.235), custom_call_target="tpu_custom_call" | custom-call | tf_op jit(solution)/shard_map/pallas_call | solution.py:118
  174.8 13.1 %shard_map.162 = (f32[3,64,384]{2,1,0:T(8,128)S(1)}, f32[3,1,384]{2,1,0:T(1,128)S(1)}) custom-call(bf16[3,384,64]{2,1,0:T(8,128)(2,1)S(1)} %bitcast.216, bf16[4096,384]{1,0:T(8,128)(2,1)} %bitcast.204, s32[4096,1]{1,0:T(8,128)S(1)} %copy.176.kpos_ref, s32[1,384]{1,0:T(1,128)S(1)} %bitcast.239), custom_call_target="tpu_custom_call" | custom-call | tf_op jit(solution)/shard_map/pallas_call | solution.py:238
  195.0 10.4 %shard_map.163 = bf16[4,128,576]{2,1,0:T(8,128)(2,1)S(1)} custom-call(bf16[128,576]{1,0:T(8,128)(2,1)S(1)} %multiply_convert_fusion.6.x_ref), custom_call_target="tpu_custom_call" | custom-call | tf_op jit(solution)/shard_map/pallas_call | solution.py:118
  216.6 10.2 %shard_map.164 = bf16[4,128,576]{2,1,0:T(8,128)(2,1)S(1)} custom-call(bf16[4,128,576]{2,1,0:T(8,128)(2,1)S(1)} %copy-done.13), custom_call_target="tpu_custom_call" | custom-call | tf_op jit(solution)/shard_map/pallas_call | solution.py:118
  233.2 9.9 %shard_map.165 = bf16[4,128,576]{2,1,0:T(8,128)(2,1)S(1)} custom-call(bf16[4,128,576]{2,1,0:T(8,128)(2,1)S(1)} %bitcast.228), custom_call_target="tpu_custom_call" | custom-call | tf_op jit(solution)/shard_map/pallas_call | solution.py:118
  251.6 17.8 %shard_map.166 = (f32[3,64,384]{2,1,0:T(8,128)S(1)}, bf16[4096,384]{1,0:T(8,128)(2,1)}) custom-call(bf16[3,384,64]{2,1,0:T(8,128)(2,1)S(1)} %bitcast.217, bf16[3,384,64]{2,1,0:T(8,128)(2,1)S(1)} %bitcast.237, bf16[4096,384]{1,0:T(8,128)(2,1)} %bitcast.205, s32[4096,1]{1,0:T(8,128)S(1)} %copy.176.kpos_ref, s32[1,384]{1,0:T(1,128)S(1)} %bitcast.240, ...), custom_call_target="tpu_custom_call" | custom-call | tf_op jit(solution)/shard_map/pallas_call | solution.py:238
  282.7 20.5 %shard_map.168 = bf16[4,512,384]{2,1,0:T(8,128)(2,1)S(1)} custom-call(bf16[4,512,384]{2,1,0:T(8,128)(2,1)S(1)} %bitcast.206), custom_call_target="tpu_custom_call" | custom-call | tf_op jit(solution)/shard_map/pallas_call | solution.py:118
  307.9 12.1 %shard_map.169 = bf16[4,128,384]{2,1,0:T(8,128)(2,1)S(1)} custom-call(bf16[4,128,384]{2,1,0:T(8,128)(2,1)S(1)} %bitcast.232), custom_call_target="tpu_custom_call" | custom-call | tf_op jit(solution)/shard_map/pallas_call | solution.py:118
  344.7 20.2 %shard_map.171 = bf16[4,160,1536]{2,1,0:T(8,128)(2,1)S(1)} custom-call(bf16[4,160,1536]{2,1,0:T(8,128)(2,1)S(1)} %fusion.1.x_ref), custom_call_target="tpu_custom_call" | custom-call | tf_op jit(solution)/shard_map/pallas_call | solution.py:118
  374.0 9.6 %shard_map.172 = bf16[4,128,576]{2,1,0:T(8,128)(2,1)S(1)} custom-call(bf16[4,128,576]{2,1,0:T(8,128)(2,1)S(1)} %bitcast.229), custom_call_target="tpu_custom_call" | custom-call | tf_op jit(solution)/shard_map/pallas_call | solution.py:118
  386.5 17.8 %shard_map.173 = (f32[3,64,384]{2,1,0:T(8,128)S(1)}, bf16[4096,384]{1,0:T(8,128)(2,1)}) custom-call(bf16[3,384,64]{2,1,0:T(8,128)(2,1)S(1)} %bitcast.215, bf16[3,384,64]{2,1,0:T(8,128)(2,1)S(1)} %bitcast.236, bf16[4096,384]{1,0:T(8,128)(2,1)} %bitcast.203, s32[4096,1]{1,0:T(8,128)S(1)} %copy.176.kpos_ref, s32[1,384]{1,0:T(1,128)S(1)} %bitcast.241, ...), custom_call_target="tpu_custom_call" | custom-call | tf_op jit(solution)/shard_map/pallas_call | solution.py:238
  413.3 20.8 %shard_map.175 = bf16[4,512,384]{2,1,0:T(8,128)(2,1)S(1)} custom-call(bf16[4,512,384]{2,1,0:T(8,128)(2,1)S(1)} %bitcast.207), custom_call_target="tpu_custom_call" | custom-call | tf_op jit(solution)/shard_map/pallas_call | solution.py:118
  434.6 14.9 %shard_map.176 = bf16[4,128,384]{2,1,0:T(8,128)(2,1)S(1)} custom-call(bf16[4,128,384]{2,1,0:T(8,128)(2,1)S(1)} %bitcast.233), custom_call_target="tpu_custom_call" | custom-call | tf_op jit(solution)/shard_map/pallas_call | solution.py:118
  457.1 21.3 %shard_map.178 = bf16[4,160,1536]{2,1,0:T(8,128)(2,1)S(1)} custom-call(bf16[4,160,1536]{2,1,0:T(8,128)(2,1)S(1)} %fusion.x_ref), custom_call_target="tpu_custom_call" | custom-call | tf_op jit(solution)/shard_map/pallas_call | solution.py:118
  479.3 16.9 %shard_map.179 = bf16[8,240,128]{2,1,0:T(8,128)(2,1)S(1)} custom-call(bf16[8,240,128]{2,1,0:T(8,128)(2,1)S(1)} %bitcast.230), custom_call_target="tpu_custom_call" | custom-call | tf_op jit(solution)/shard_map/pallas_call | solution.py:118
  496.2 18.6 %shard_map.180 = bf16[8,240,128]{2,1,0:T(8,128)(2,1)S(1)} custom-call(bf16[240,128]{1,0:T(8,128)(2,1)S(1)} %reduce_sum.287.x_ref), custom_call_target="tpu_custom_call" | custom-call | tf_op jit(solution)/shard_map/pallas_call | solution.py:118
  515.8 18.1 %shard_map.177 = bf16[4,2,128,576]{3,2,1,0:T(8,128)(2,1)S(1)} custom-call(bf16[2,128,576]{2,1,0:T(8,128)(2,1)S(1)} %pad_maximum_fusion.4.x_ref), custom_call_target="tpu_custom_call" | custom-call | tf_op jit(solution)/shard_map/pallas_call | solution.py:118
  (345 shorter events, 168.8 us)
Async XLA Ops:
  7.2 91.1 %all-gather.2.cloned.1.call-start = ((), (), s32[]{:S(2)}) async-start(), calls=%async_computation | async-start | bytes 3133440 | tf_op jit(solution)/shard_map/all_gather | solution.py:309
  10.4 26.0 %copy-start.70 = (bf16[2,576]{1,0:T(2,128)(2,1)S(1)}, bf16[2,576]{1,0:T(2,128)(2,1)}, u32[]{:S(2)}) copy-start(bf16[2,576]{1,0:T(2,128)(2,1)} %param.11) | copy-start | bytes 6916
  10.5 534.1 %all-reduce.3.cloned.1.call-start = ((), (), s32[]{:S(2)}) async-start(), calls=%async_computation.1 | async-start | bytes 6291456 | tf_op jit(solution)/shard_map/psum | solution.py:384
  12.0 86.3 %copy-start.23 = (bf16[128,576]{1,0:T(8,128)(2,1)}, bf16[128,576]{1,0:T(8,128)(2,1)S(1)}, u32[]{:S(2)}) copy-start(bf16[128,576]{1,0:T(8,128)(2,1)S(1)} %copy.220) | copy-start | bytes 442372
  36.5 93.5 %copy-start.68 = (f32[576]{0:T(1024)}, f32[576]{0:T(1024)S(1)}, u32[]{:S(2)}) copy-start(f32[576]{0:T(1024)S(1)} %get-tuple-element.78) | copy-start | bytes 6916
  80.5 14.9 %copy-start.71 = (bf16[2,576]{1,0:T(2,128)(2,1)S(1)}, bf16[2,576]{1,0:T(2,128)(2,1)}, u32[]{:S(2)}) copy-start(bf16[2,576]{1,0:T(2,128)(2,1)} %param.14) | copy-start | bytes 6916
  95.4 4.5 copy-start.35
  95.5 4.5 copy-start.66
  98.3 13.6 %copy-start.32 = (bf16[2,2,576,384]{3,2,1,0:T(8,128)(2,1)S(1)}, bf16[2,2,576,384]{3,2,1,0:T(8,128)(2,1)}, u32[]{:S(2)}) copy-start(bf16[2,2,576,384]{3,2,1,0:T(8,128)(2,1)} %param.15) | copy-start | bytes 5308420
  100.0 13.8 %copy-start.75 = (f32[128]{0:T(128)}, f32[128]{0:T(128)S(1)}, u32[]{:S(2)}) copy-start(f32[128]{0:T(128)S(1)} %add_rsqrt_fusion.2) | copy-start | bytes 1540
  119.1 10.1 %copy-start.21 = (f32[128,576]{1,0:T(8,128)S(1)}, f32[128,576]{1,0:T(8,128)}, u32[]{:S(2)}) copy-start(f32[128,576]{1,0:T(8,128)} %copy-done.20) | copy-start | bytes 884740
  192.2 13.3 %copy-start.33 = (bf16[2,2,576,384]{3,2,1,0:T(8,128)(2,1)S(1)}, bf16[2,2,576,384]{3,2,1,0:T(8,128)(2,1)}, u32[]{:S(2)}) copy-start(bf16[2,2,576,384]{3,2,1,0:T(8,128)(2,1)} %param.15) | copy-start | bytes 5308420
  194.2 11.8 %copy-start.80 = (f32[512,384]{1,0:T(8,128)S(1)}, f32[512,384]{1,0:T(8,128)}, u32[]{:S(2)}) copy-start(f32[512,384]{1,0:T(8,128)} %fusion.19) | copy-start | bytes 2359300
  216.6 11.0 %copy-start.31 = (f32[512,576]{0,1:T(8,128)S(1)}, f32[512,576]{0,1:T(8,128)}, u32[]{:S(2)}) copy-start(f32[512,576]{0,1:T(8,128)} %fusion.24) | copy-start | bytes 3538948
  216.6 11.0 %copy-start.64 = (bf16[512,384]{1,0:T(8,128)(2,1)S(1)}, bf16[512,384]{1,0:T(8,128)(2,1)}, u32[]{:S(2)}) copy-start(bf16[512,384]{1,0:T(8,128)(2,1)} %copy-done.63) | copy-start | bytes 1179652
  233.2 10.0 %copy-start.30 = (f32[128,576]{1,0:T(8,128)S(1)}, f32[128,576]{1,0:T(8,128)}, u32[]{:S(2)}) copy-start(f32[128,576]{1,0:T(8,128)} %copy-done.29) | copy-start | bytes 884740
  233.2 10.0 %copy-start.49 = (f32[128,576]{1,0:T(8,128)S(1)}, f32[128,576]{1,0:T(8,128)}, u32[]{:S(2)}) copy-start(f32[128,576]{1,0:T(8,128)} %convert_reduce_fusion.3) | copy-start | bytes 884740
  233.2 11.4 %copy-start.58 = (bf16[128,576]{1,0:T(8,128)(2,1)S(1)}, bf16[128,576]{1,0:T(8,128)(2,1)}, u32[]{:S(2)}) copy-start(bf16[128,576]{1,0:T(8,128)(2,1)} %copy.221) | copy-start | bytes 442372
  304.4 16.4 %copy-start.18 = (f32[3,64,384]{2,1,0:T(8,128)S(1)}, f32[3,64,384]{2,1,0:T(8,128)}, u32[]{:S(2)}) copy-start(f32[3,64,384]{2,1,0:T(8,128)} %copy-done.17) | copy-start | bytes 884740
  330.9 11.7 %copy-start.72 = (bf16[576]{0:T(1024)(128)(2,1)S(1)}, bf16[576]{0:T(1024)(128)(2,1)}, u32[]{:S(2)}) copy-start(bf16[576]{0:T(1024)(128)(2,1)} %get-tuple-element.70) | copy-start | bytes 3460
  372.6 11.2 %copy-start.22 = (f32[128,576]{1,0:T(8,128)S(1)}, f32[128,576]{1,0:T(8,128)}, u32[]{:S(2)}) copy-start(f32[128,576]{1,0:T(8,128)} %copy-done.20) | copy-start | bytes 884740
  372.6 11.2 %copy-start.67 = (f32[576]{0:T(1024)S(1)}, f32[576]{0:T(1024)}, u32[]{:S(2)}) copy-start(f32[576]{0:T(1024)} %copy-done.66) | copy-start | bytes 6916
  372.6 11.2 %copy-start.76 = (f32[128]{0:T(128)S(1)}, f32[128]{0:T(128)}, u32[]{:S(2)}) copy-start(f32[128]{0:T(128)} %copy-done.75) | copy-start | bytes 1540
  374.0 9.9 %copy-start.48 = (f32[128,576]{1,0:T(8,128)S(1)}, f32[128,576]{1,0:T(8,128)}, u32[]{:S(2)}) copy-start(f32[128,576]{1,0:T(8,128)} %get-tuple-element.84) | copy-start | bytes 884740
  (60 other events, 106.5 us)
Sparse Core Ops, SparseCore 0:
  10.6 59.9 all-gather.1
  453.9 90.6 all-reduce.2
